TPU v7x, 32 devices: a whole 2x2x4 slice. The times are simulated.
32 devices in a mesh: grp: 2 (over x), leaf: 8 (over z, y), sub: 2 (over core).
Axes of the slice: x: 2, y: 2, z: 4, core: 2. Of those that a mesh axis runs over, the one named last changes fastest.
Arguments:
- right_side: float32 [512, 2048], P(('grp', 'leaf', 'sub')), parts along dimension 0, may hold values from -24 to 24, as said below
- first_guess: float32 [512, 2048], P(('grp', 'leaf', 'sub')), parts along dimension 0, may hold values from -3 to 3
- couple: bfloat16 [512, 64, 384], P(('grp', 'leaf', 'sub')), parts along dimension 0, may hold values from -0.75 to 0.75
- send_lists: int32 [32, 2, 4], P(('grp', 'leaf', 'sub')), parts along dimension 0, may hold values from -1 to 15, as said below
- neighbours: int32 [512, 6], P(('grp', 'leaf', 'sub')), parts along dimension 0, may hold values from -1 to 23, as said below
Outputs:
- solution: float32 [512, 2048], P(('grp', 'leaf', 'sub')), parts along dimension 0
- residual: float32 [512, 2048], P(('grp', 'leaf', 'sub')), parts along dimension 0
There are 2 independent parts, one for each index of `grp`. A program takes and returns all parts, laid end to end along the dimension named above; each array names one. Nothing has to cross between parts.
Inputs may be any that keep to these rules, and one draw needn't show every extreme that they name: `right_side`: rows rise in scale along the element order. `send_lists`: for device d of a part and direction 0 (toward device d + 1) or 1 (toward device d - 1): distinct local element indices in the live slots, which come first, and -1 after them. The first device sends nothing in direction 1, the last nothing in direction 0; some device fills all 4 slots in direction 0 and the device after it all 4 in direction 1. `neighbours`: positions below 16 are the device's own elements, 16 + s the live slot s received from the previous device, 20 + s the live slot s received from the next device; -1 marks a face on the band's boundary.
All inputs are finite; a program needn't handle non-finite values.
Results may differ from a plain program's by a relative error of at most 0.034.
Values may be sent and summed in bfloat16 or wider, within the bound.
No kernel may reach another device: no remote copies, remote signals or barrier semaphores. Data moves between devices by JAX's collectives and lax.ppermute only.
A program may use at most 64 MiB of HBM per device.

v0:
```python
import jax
import jax.numpy as jnp
from jax import lax
from jax.sharding import PartitionSpec as P

DOF = 64
FACES = 6
RHS = 32
SSTEP = 3
CYCLES = 4


def from_behind(value, axis, steps):
    count = lax.axis_size(axis)
    first, last = (max(0, -steps), min(count, count - steps))
    return lax.ppermute(value, axis, [(source, source + steps) for source in range(first, last)])


def couple_apply(vector_field, couple, send_lists, neighbours):
    local_count = vector_field.shape[0]
    slot_count = send_lists.shape[2]
    row_width = vector_field.shape[1]
    halves = vector_field.astype(jnp.bfloat16)
    own_lists = send_lists[0]
    chosen = jnp.take(halves, jnp.maximum(own_lists, 0).reshape(-1), axis=0).reshape(
        2, slot_count, row_width
    )
    chosen = jnp.where(own_lists[:, :, None] >= 0, chosen, jnp.zeros_like(chosen))
    forward = chosen[0]
    backward = chosen[1]
    before_blocks = from_behind(forward, ("leaf", "sub"), 1)
    after_blocks = from_behind(backward, ("leaf", "sub"), -1)
    zero_block = jnp.zeros((1, row_width), jnp.bfloat16)
    extended = jnp.concatenate([halves, before_blocks, after_blocks, zero_block], axis=0)
    positions = jnp.where(neighbours < 0, local_count + 2 * slot_count, neighbours).reshape(-1)
    gathered = jnp.take(extended, positions, axis=0).reshape(local_count, FACES * DOF, RHS)
    product = jnp.einsum("eik,ekr->eir", couple, gathered, preferred_element_type=jnp.float32)
    return product.reshape(local_count, DOF * RHS)


def to_columns(vector_field):
    return vector_field.reshape(-1, RHS)


def basis_sums(stacked):
    partial_sum = jnp.dot(
        stacked.T, stacked, precision=lax.Precision.HIGHEST, preferred_element_type=jnp.float32
    )
    total_sum = lax.psum(partial_sum, ("leaf", "sub"))
    return (total_sum[: SSTEP * RHS, : SSTEP * RHS], total_sum[: SSTEP * RHS, SSTEP * RHS :])


def shards(right_side, first_guess, couple, send_lists, neighbours):
    solution = first_guess
    residual = right_side - first_guess + couple_apply(first_guess, couple, send_lists, neighbours)
    for repeat in range(CYCLES):
        krylov_blocks = [residual]
        for degree in range(SSTEP):
            krylov_blocks.append(couple_apply(krylov_blocks[-1], couple, send_lists, neighbours))
        images = [
            krylov_blocks[order_index] - krylov_blocks[order_index + 1]
            for order_index in range(SSTEP)
        ]
        stacked = jnp.concatenate(
            [to_columns(image_block) for image_block in images] + [to_columns(residual)], axis=1
        )
        square_block, right_block = basis_sums(stacked)
        factor = jnp.linalg.cholesky(square_block)
        coeffs = jax.scipy.linalg.cho_solve((factor, True), right_block)
        krylov = jnp.concatenate(
            [to_columns(basis_block) for basis_block in krylov_blocks[:SSTEP]], axis=1
        )
        solution = solution + jnp.dot(
            krylov, coeffs, precision=lax.Precision.HIGHEST, preferred_element_type=jnp.float32
        ).reshape(solution.shape)
        residual = residual - jnp.dot(
            stacked[:, : SSTEP * RHS],
            coeffs,
            precision=lax.Precision.HIGHEST,
            preferred_element_type=jnp.float32,
        ).reshape(residual.shape)
    return (solution, residual)


def solution(mesh):
    placed = (
        P(("grp", "leaf", "sub"), None),
        P(("grp", "leaf", "sub"), None),
        P(("grp", "leaf", "sub"), None, None),
        P(("grp", "leaf", "sub"), None, None),
        P(("grp", "leaf", "sub"), None),
    )
    return jax.shard_map(
        shards,
        mesh=mesh,
        in_specs=placed,
        out_specs=(P(("grp", "leaf", "sub"), None), P(("grp", "leaf", "sub"), None)),
        check_vma=False,
    )
```

profile of v0, /device:TPU:0, one launch (start us, length us, event | category | flops | bytes accessed | tf_op | source)
XLA Modules:
  0.0 678.5 jit_solution(5330621828256337347)
XLA Ops:
  15.2 2.9 collective-permute-done.1
  22.3 4.4 collective-permute-start.2
  36.3 4.7 collective-permute-start.4
  50.1 4.8 collective-permute-start.6
  65.5 87.5 %all-reduce.5.cloned.1.call-done = f32[128,128]{0,1:T(8,128)} async-done(((f32[128,128]{0,1:T(8,128)}), f32[128,128]{0,1:T(8,128)}) %all-reduce.5.cloned.1.call-update) | async-done | bytes 65552 | tf_op jit(solution)/shard_map/psum | solution.py:49
  154.8 8.8 %cholesky.74 = f32[96,96]{1,0:T(8,128)S(1)} custom-call(f32[96,96]{1,0:T(8,128)S(1)} %fusion.103), custom_call_target="Cholesky" | custom-call | tf_op jit(solution)/shard_map/jit(cholesky)/cholesky | solution.py:68
  164.9 7.4 %custom-call.10 = f32[1,96,96]{1,2,0:T(8,128)S(1)} custom-call(f32[1,96,96]{2,1,0:T(8,128)S(1)} %fusion.80), custom_call_target="InvertDiagBlocksLowerTriangular" | custom-call | tf_op jit(solution)/shard_map/jit(_cho_solve)/triangular_solve | solution.py:69
  186.2 4.4 collective-permute-start.10
  192.3 3.1 collective-permute-done.11
  205.0 6.0 collective-permute-start.12
  223.6 86.4 %all-reduce.7.cloned.1.call-done = f32[128,128]{0,1:T(8,128)} async-done(((f32[128,128]{0,1:T(8,128)}), f32[128,128]{0,1:T(8,128)}) %all-reduce.7.cloned.1.call-update) | async-done | bytes 65552 | tf_op jit(solution)/shard_map/psum | solution.py:49
  311.7 8.8 %cholesky.85 = f32[96,96]{1,0:T(8,128)S(1)} custom-call(f32[96,96]{1,0:T(8,128)S(1)} %fusion.98), custom_call_target="Cholesky" | custom-call | tf_op jit(solution)/shard_map/jit(cholesky)/cholesky | solution.py:68
  321.8 7.4 %custom-call.11 = f32[1,96,96]{1,2,0:T(8,128)S(1)} custom-call(f32[1,96,96]{2,1,0:T(8,128)S(1)} %fusion.81), custom_call_target="InvertDiagBlocksLowerTriangular" | custom-call | tf_op jit(solution)/shard_map/jit(_cho_solve)/triangular_solve | solution.py:69
  347.3 4.4 collective-permute-start.16
  353.0 3.5 collective-permute-done.17
  366.2 6.0 collective-permute-start.18
  385.2 86.2 %all-reduce.9.cloned.1.call-done = f32[128,128]{0,1:T(8,128)} async-done(((f32[128,128]{0,1:T(8,128)}), f32[128,128]{0,1:T(8,128)}) %all-reduce.9.cloned.1.call-update) | async-done | bytes 65552 | tf_op jit(solution)/shard_map/psum | solution.py:49
  473.1 8.8 %cholesky.96 = f32[96,96]{1,0:T(8,128)S(1)} custom-call(f32[96,96]{1,0:T(8,128)S(1)} %fusion.93), custom_call_target="Cholesky" | custom-call | tf_op jit(solution)/shard_map/jit(cholesky)/cholesky | solution.py:68
  483.3 7.4 %custom-call.12 = f32[1,96,96]{1,2,0:T(8,128)S(1)} custom-call(f32[1,96,96]{2,1,0:T(8,128)S(1)} %fusion.82), custom_call_target="InvertDiagBlocksLowerTriangular" | custom-call | tf_op jit(solution)/shard_map/jit(_cho_solve)/triangular_solve | solution.py:69
  511.1 4.3 collective-permute-start.22
  532.4 5.3 collective-permute-start.24
  561.6 86.0 %all-reduce.11.cloned.1.call-done = f32[128,128]{0,1:T(8,128)} async-done(((f32[128,128]{0,1:T(8,128)}), f32[128,128]{0,1:T(8,128)}) %all-reduce.11.cloned.1.call-update) | async-done | bytes 65552 | tf_op jit(solution)/shard_map/psum | solution.py:49
  649.3 8.8 %cholesky.107 = f32[96,96]{1,0:T(8,128)S(1)} custom-call(f32[96,96]{1,0:T(8,128)S(1)} %fusion.88), custom_call_target="Cholesky" | custom-call | tf_op jit(solution)/shard_map/jit(cholesky)/cholesky | solution.py:68
  659.4 7.4 %custom-call.13 = f32[1,96,96]{1,2,0:T(8,128)S(1)} custom-call(f32[1,96,96]{2,1,0:T(8,128)S(1)} %fusion.83), custom_call_target="InvertDiagBlocksLowerTriangular" | custom-call | tf_op jit(solution)/shard_map/jit(_cho_solve)/triangular_solve | solution.py:69
  (484 shorter events, 197.7 us)
Async XLA Ops:
  7.2 145.9 %all-reduce.5.cloned.1.call-start = ((), (), s32[]{:S(2)}) async-start(), calls=%async_computation | async-start | bytes 131072 | tf_op jit(solution)/shard_map/psum | solution.py:49
  10.5 4.7 collective-permute-start
  12.9 5.2 collective-permute-start.1
  22.3 5.7 collective-permute-start.2
  36.3 6.0 collective-permute-start.4
  50.1 8.9 %collective-permute-start.6 = (bf16[4,2048]{1,0:T(4,128)(2,1)S(1)}, bf16[4,2048]{1,0:T(4,128)(2,1)S(1)}, u32[]{:S(2)}, u32[]{:S(2)}) collective-permute-start(bf16[4,2048]{1,0:T(4,128)(2,1)S(1)} %get-tuple-element.48), channel_id=1, source_target_pairs={{0,1},{1,2},{2,3},{3,4},{4,5},{5,6},{6,7},{7,8},{8,9},{9,10},{10,1... | collective-permute-start | bytes 49160 | tf_op jit(solution)/shard_map/ppermute | solution.py:16
  54.9 4.1 collective-permute-start.7
  65.5 244.5 %all-reduce.7.cloned.1.call-start = ((), (), s32[]{:S(2)}) async-start(), calls=%async_computation.1 | async-start | bytes 131072 | tf_op jit(solution)/shard_map/psum | solution.py:49
  186.2 6.1 collective-permute-start.10
  190.6 4.8 collective-permute-start.11
  205.0 11.2 %collective-permute-start.12 = (bf16[4,2048]{1,0:T(4,128)(2,1)}, bf16[4,2048]{1,0:T(4,128)(2,1)S(1)}, u32[]{:S(2)}, u32[]{:S(2)}) collective-permute-start(bf16[4,2048]{1,0:T(4,128)(2,1)} %get-tuple-element.42), channel_id=1, source_target_pairs={{0,1},{1,2},{2,3},{3,4},{4,5},{5,6},{6,7},{7,8},{8,9},{9,10},{10,1... | collective-permute-start | bytes 49160 | tf_op jit(solution)/shard_map/ppermute | solution.py:16
  211.0 5.2 collective-permute-start.13
  223.5 247.9 %all-reduce.9.cloned.1.call-start = ((), (), s32[]{:S(2)}) async-start(), calls=%async_computation.2 | async-start | bytes 131072 | tf_op jit(solution)/shard_map/psum | solution.py:49
  333.1 3.7 collective-permute-start.14
  347.3 5.7 collective-permute-start.16
  351.7 4.8 collective-permute-start.17
  366.2 11.5 %collective-permute-start.18 = (bf16[4,2048]{1,0:T(4,128)(2,1)}, bf16[4,2048]{1,0:T(4,128)(2,1)S(1)}, u32[]{:S(2)}, u32[]{:S(2)}) collective-permute-start(bf16[4,2048]{1,0:T(4,128)(2,1)} %get-tuple-element.36), channel_id=1, source_target_pairs={{0,1},{1,2},{2,3},{3,4},{4,5},{5,6},{6,7},{7,8},{8,9},{9,10},{10,1... | collective-permute-start | bytes 49160 | tf_op jit(solution)/shard_map/ppermute | solution.py:16
  372.2 5.5 collective-permute-start.19
  385.0 262.6 %all-reduce.11.cloned.1.call-start = ((), (), s32[]{:S(2)}) async-start(), calls=%async_computation.3 | async-start | bytes 131072 | tf_op jit(solution)/shard_map/psum | solution.py:49
  494.0 5.6 collective-permute-start.20
  511.1 11.6 %collective-permute-start.22 = (bf16[4,2048]{1,0:T(4,128)(2,1)S(1)}, bf16[4,2048]{1,0:T(4,128)(2,1)S(1)}, u32[]{:S(2)}, u32[]{:S(2)}) collective-permute-start(bf16[4,2048]{1,0:T(4,128)(2,1)S(1)} %get-tuple-element.32), channel_id=1, source_target_pairs={{0,1},{1,2},{2,3},{3,4},{4,5},{5,6},{6,7},{7,8},{8,9},{9,10},{10,1... | collective-permute-start | bytes 49160 | tf_op jit(solution)/shard_map/ppermute | solution.py:16
  515.4 7.2 %collective-permute-start.23 = (bf16[4,2048]{1,0:T(4,128)(2,1)S(1)}, bf16[4,2048]{1,0:T(4,128)(2,1)S(1)}, u32[]{:S(2)}, u32[]{:S(2)}) collective-permute-start(bf16[4,2048]{1,0:T(4,128)(2,1)S(1)} %get-tuple-element.33), channel_id=1, source_target_pairs={{1,0},{2,1},{3,2},{4,3},{5,4},{6,5},{7,6},{8,7},{9,8},{10,9},{11,1... | collective-permute-start | bytes 49160 | tf_op jit(solution)/shard_map/ppermute | solution.py:16
  532.4 15.2 %collective-permute-start.24 = (bf16[4,2048]{1,0:T(4,128)(2,1)}, bf16[4,2048]{1,0:T(4,128)(2,1)}, u32[]{:S(2)}, u32[]{:S(2)}) collective-permute-start(bf16[4,2048]{1,0:T(4,128)(2,1)} %get-tuple-element.30), channel_id=1, source_target_pairs={{0,1},{1,2},{2,3},{3,4},{4,5},{5,6},{6,7},{7,8},{8,9},{9,10},{10,1... | collective-permute-start | bytes 49160 | tf_op jit(solution)/shard_map/ppermute | solution.py:16
  537.7 9.9 %collective-permute-start.25 = (bf16[4,2048]{1,0:T(4,128)(2,1)}, bf16[4,2048]{1,0:T(4,128)(2,1)}, u32[]{:S(2)}, u32[]{:S(2)}) collective-permute-start(bf16[4,2048]{1,0:T(4,128)(2,1)} %get-tuple-element.31), channel_id=1, source_target_pairs={{1,0},{2,1},{3,2},{4,3},{5,4},{6,5},{7,6},{8,7},{9,8},{10,9},{11,1... | collective-permute-start | bytes 49160 | tf_op jit(solution)/shard_map/ppermute | solution.py:16
  (86 other events, 1717.7 us)
Sparse Core Ops, SparseCore 0:
  65.6 87.4 all-reduce.4
  223.6 86.2 all-reduce.6
  385.1 86.2 all-reduce.8
  557.8 89.6 all-reduce.10
where the time goes:
time: 688 us; the launch traced here: 679 us
  waiting for transfers between devices  363 us (53%)
  other arithmetic  104 us (15%)
  local copies, waits for them, and re-layouts  94.6 us (14%)
  starting transfers between devices  71.7 us (10%)
  matrix products  28.9 us (4%)
  between operations  16.5 us (2%)
    psum x4, waiting for transfers between devices, basis_sums(): total_sum = lax.psum(partial_sum, ('leaf', 'sub'))  346 us
    ppermute x26, starting transfers between devices, from_behind(): lax.ppermute(value, axis, [(source, source + steps) for source in range(f...  71.3 us
    another operation x12, other arithmetic, shards(): factor = jnp.linalg.cholesky(square_block)  37.9 us
    another operation x8, other arithmetic, shards(): coeffs = jax.scipy.linalg.cho_solve((factor, True), right_block)  32 us
    reshape x13, local copies, waits for them, and re-layouts, couple_apply(): jnp.take(extended, positions, axis=0).reshape(local_count, FACES * DOF, RHS)  27.4 us
    ppermute x26, waiting for transfers between devices, from_behind(): lax.ppermute(value, axis, [(source, source + steps) for source in range(f...  17 us
  transfers between devices with their start and end apart: 30, of which 11 were waited for; matrix products, arithmetic and copies ran while one was open for 5% of the time, Pallas kernels for 0%

commit v1 on v0

v1 whole, which is shorter than its diff:
```python
import functools

import jax
import jax.numpy as jnp
from jax import lax
from jax.experimental import pallas as pl
from jax.experimental.pallas import tpu as pltpu
from jax.sharding import PartitionSpec as P

DOF = 64
FACES = 6
RHS = 32
SSTEP = 3
CYCLES = 4
AXES = ("leaf", "sub")
F32 = jnp.float32
BF16 = jnp.bfloat16

VMEM = pl.BlockSpec(memory_space=pltpu.VMEM)
SMEM = pl.BlockSpec(memory_space=pltpu.SMEM)
PARAMS = pltpu.CompilerParams(vmem_limit_bytes=16 * 1024 * 1024)


def fill_extended(ext, own, from_chip, from_link):
    count, slots = own.shape[0], from_chip.shape[0]
    ext[:count] = own[...]
    ext[count : count + slots] = from_chip[...]
    ext[count + slots : count + 2 * slots] = from_link[...]
    ext[count + 2 * slots] = jnp.zeros(ext.shape[1:], BF16)


def coupled(e, positions, couple, ext):
    gathered = jnp.concatenate([ext[positions[e, f]] for f in range(FACES)], axis=0)
    return jnp.dot(couple[e], gathered, preferred_element_type=F32)


def pick_sends(lists, ext, to_chip, to_link):
    for s in range(to_chip.shape[0]):
        to_chip[s] = ext[lists[0, s]]
        to_link[s] = ext[lists[1, s]]


def split(value):
    high = value.astype(BF16)
    return high, (value - high.astype(F32)).astype(BF16)


def start_kernel(lists, x, own, to_chip, to_link, ext):
    own[...] = x[...].astype(BF16)
    ext[: x.shape[0]] = own[...]
    ext[x.shape[0]] = jnp.zeros(ext.shape[1:], BF16)
    pick_sends(lists, ext, to_chip, to_link)


def residual_kernel(lists, positions, couple, own, from_chip, from_link, b, x, r, new_own, to_chip, to_link, ext):
    count = own.shape[0]
    fill_extended(ext, own, from_chip, from_link)
    for e in range(count):
        value = b[e] - x[e] + coupled(e, positions, couple, ext)
        r[e] = value
        new_own[e] = value.astype(BF16)
    ext[:count] = new_own[...]
    ext[count] = jnp.zeros(ext.shape[1:], BF16)
    pick_sends(lists, ext, to_chip, to_link)


def power_kernel(lists, positions, couple, own, from_chip, from_link, power, new_own, to_chip, to_link, ext):
    count = own.shape[0]
    fill_extended(ext, own, from_chip, from_link)
    for e in range(count):
        value = coupled(e, positions, couple, ext)
        power[e] = value
        new_own[e] = value.astype(BF16)
    ext[:count] = new_own[...]
    ext[count] = jnp.zeros(ext.shape[1:], BF16)
    pick_sends(lists, ext, to_chip, to_link)


def gram_kernel(positions, couple, own, from_chip, from_link, b0, b1, b2, last, gram, ext):
    count = own.shape[0]
    rows = count * DOF
    fill_extended(ext, own, from_chip, from_link)
    for e in range(count):
        last[e] = coupled(e, positions, couple, ext)
    fields = [field[...].reshape(rows, RHS) for field in (b0, b1, b2, last)]
    stacked = jnp.concatenate([fields[k] - fields[k + 1] for k in range(SSTEP)] + [fields[0]], axis=1)
    high, low = split(stacked)
    sums = lax.dot_general(
        high, jnp.concatenate([high, low], axis=1), (((0,), (0,)), ((), ())), preferred_element_type=F32
    )
    width = stacked.shape[1]
    cross = sums[:, width:]
    gram[...] = sums[:, :width] + cross + cross.T


def eliminate(gram):
    size = SSTEP * RHS
    groups = [gram[8 * g : 8 * g + 8, :] for g in range(size // 8)]
    row_ids = lax.broadcasted_iota(jnp.int32, groups[0].shape, 0)
    for j in range(size):
        home, place = divmod(j, 8)
        row = groups[home][place : place + 1, :]
        scaled = row / row[:, j : j + 1]
        for g in range(size // 8):
            updated = groups[g] - groups[g][:, j : j + 1] * scaled
            groups[g] = jnp.where(row_ids == place, scaled, updated) if g == home else updated
    return jnp.concatenate(groups, axis=0)


def update_values(gram, b0, b1, b2, b3, x):
    count = x.shape[0]
    rows = count * DOF
    reduced = eliminate(gram)
    width = reduced.shape[1]
    zeros = jnp.zeros((RHS, width), F32)
    lanes = lax.broadcasted_iota(jnp.int32, (width, width), 1)
    rows_at = lax.broadcasted_iota(jnp.int32, (width, width), 0)
    sol = jnp.concatenate([reduced, zeros], axis=0)
    res = jnp.concatenate([zeros, reduced], axis=0) - sol
    res = res + jnp.where(lanes - (width - RHS) == rows_at, 1.0, 0.0).astype(F32)
    res = pltpu.roll(res, width - RHS, 1)
    mix = jnp.where(lanes >= width - RHS, sol, jnp.where(lanes >= width - 2 * RHS, res, 0.0))
    fields = jnp.concatenate([field[...].reshape(rows, RHS) for field in (b0, b1, b2, b3)], axis=1)
    high, low = split(fields)
    mix_high, mix_low = split(mix)
    out = jnp.dot(
        jnp.concatenate([high, low], axis=1),
        jnp.concatenate([mix_high, mix_high], axis=0),
        preferred_element_type=F32,
    ) + jnp.dot(high, mix_low, preferred_element_type=F32)
    new_x = x[...] + out[:, width - RHS :].reshape(x.shape)
    new_r = out[:, width - 2 * RHS : width - RHS].reshape(x.shape)
    return new_x, new_r


def update_kernel(lists, gram, b0, b1, b2, b3, x, new_x, new_r, new_own, to_chip, to_link, ext):
    count = x.shape[0]
    new_x[...], value = update_values(gram, b0, b1, b2, b3, x)
    new_r[...] = value
    new_own[...] = value.astype(BF16)
    ext[:count] = new_own[...]
    ext[count] = jnp.zeros(ext.shape[1:], BF16)
    pick_sends(lists, ext, to_chip, to_link)


def finish_kernel(gram, b0, b1, b2, b3, x, new_x, new_r):
    new_x[...], new_r[...] = update_values(gram, b0, b1, b2, b3, x)


def shards(right_side, first_guess, couple, send_lists, neighbours):
    count = right_side.shape[0]
    slots = send_lists.shape[2]
    devices = lax.axis_size(AXES)
    assert lax.axis_size("sub") == 2
    second = lax.axis_index("sub") == 1

    field32 = jax.ShapeDtypeStruct((count, DOF, RHS), F32)
    field16 = jax.ShapeDtypeStruct((count, DOF, RHS), BF16)
    sent = jax.ShapeDtypeStruct((slots, DOF, RHS), BF16)
    ext = pltpu.VMEM((count + 2 * slots + 1, DOF, RHS), BF16)

    def call(kernel, outs, specs, name, scratch=(ext,)):
        return pl.pallas_call(
            kernel,
            out_shape=outs,
            in_specs=specs,
            out_specs=[VMEM] * len(outs),
            scratch_shapes=list(scratch),
            compiler_params=PARAMS,
            name=name,
        )

    own_lists = jnp.where(send_lists[0] < 0, count, send_lists[0]).astype(jnp.int32)
    lists = jnp.where(second, own_lists[::-1], own_lists)
    swapped = jnp.where(neighbours < count + slots, neighbours + slots, neighbours - slots)
    placed = jnp.where(second | (neighbours < count), neighbours, swapped)
    positions = jnp.where(neighbours < 0, count + 2 * slots, placed).astype(jnp.int32)

    chip_pairs = [(d, d ^ 1) for d in range(devices)]
    link_pairs = [(d, d + 1 if d % 2 else d - 1) for d in range(devices)]
    link_pairs = [(s, t) for s, t in link_pairs if 0 <= t < devices]

    def exchange(to_chip, to_link):
        from_link = lax.ppermute(to_link, AXES, link_pairs)
        from_chip = lax.ppermute(to_chip, AXES, chip_pairs)
        return from_chip, from_link

    def total(value):
        step = 1
        while step < devices:
            value = value + lax.ppermute(value, AXES, [(d, d ^ step) for d in range(devices)])
            step *= 2
        return value

    start = call(start_kernel, [field16, sent, sent], [SMEM, VMEM], "start")
    first = call(
        residual_kernel, [field32, field16, sent, sent], [SMEM, SMEM] + [VMEM] * 6, "first_residual"
    )
    power = call(power_kernel, [field32, field16, sent, sent], [SMEM, SMEM] + [VMEM] * 4, "power")
    gram = call(
        gram_kernel,
        [field32, jax.ShapeDtypeStruct(((SSTEP + 1) * RHS, (SSTEP + 1) * RHS), F32)],
        [SMEM] + [VMEM] * 7,
        "last_power_and_gram",
    )
    update = call(update_kernel, [field32, field32, field16, sent, sent], [SMEM] + [VMEM] * 6, "solve_update")
    finish = call(finish_kernel, [field32, field32], [VMEM] * 6, "solve_finish", ())

    b = right_side.reshape(count, DOF, RHS)
    x = first_guess.reshape(count, DOF, RHS)
    own, to_chip, to_link = start(lists, x)
    r, own, to_chip, to_link = first(lists, positions, couple, own, *exchange(to_chip, to_link), b, x)
    for cycle in range(CYCLES):
        b1, own, to_chip, to_link = power(lists, positions, couple, own, *exchange(to_chip, to_link))
        b2, own, to_chip, to_link = power(lists, positions, couple, own, *exchange(to_chip, to_link))
        b3, partial = gram(positions, couple, own, *exchange(to_chip, to_link), r, b1, b2)
        sums = total(partial)
        if cycle + 1 < CYCLES:
            x, r, own, to_chip, to_link = update(lists, sums, r, b1, b2, b3, x)
        else:
            x, r = finish(sums, r, b1, b2, b3, x)
    return x.reshape(right_side.shape), r.reshape(right_side.shape)


def solution(mesh):
    rows = ("grp", "leaf", "sub")
    placed = (P(rows, None), P(rows, None), P(rows, None, None), P(rows, None, None), P(rows, None))
    return jax.shard_map(
        shards,
        mesh=mesh,
        in_specs=placed,
        out_specs=(P(rows, None), P(rows, None)),
        check_vma=False,
    )
```

time: 688 us -> 213 us (0.31); the launches traced: 679 us -> 212 us
  waiting for transfers between devices: 363 us -> 35.5 us
  other arithmetic: 104 us -> 0.16 us
  local copies, waits for them, and re-layouts: 94.6 us -> 3.89 us
  Pallas kernels: 0 us -> 57.6 us
  starting transfers between devices: 71.7 us -> 114 us
  matrix products: 28.9 us -> 0 us
  between operations: 16.5 us -> 1.07 us
    psum x4 -> x0, waiting for transfers between devices: 346 us -> none  [basis_sums(): total_sum = lax.psum(partial_sum, ('leaf', 'sub'))]
    another operation x20 -> x0, other arithmetic: 69.9 us -> none  [the longest x12 37.9 us: shards(): factor = jnp.linalg.cholesky(square_block)]
    pallas_call x0 -> x18, Pallas kernels: none -> 57.6 us  [the longest x3 29.7 us: shards(): x, r, own, to_chip, to_link = update(lists, sums, r, b1, b2, b3, x)]
    ppermute x26 -> x42, starting transfers between devices: 71.3 us -> 114 us  [the longest x16 57.2 us: total(): lax.ppermute(value, AXES, [(d, d ^ step) for d in range(devices)])]
    reshape x60 -> x4, local copies, waits for them, and re-layouts: 43.6 us -> 3.09 us  [the longest x2 1.78 us: shards(): return (x.reshape(right_side.shape), r.reshape(right_side.shape))]
    dot_general x25 -> x0, matrix products: 24.7 us -> none  [the longest x13 11.1 us: couple_apply(): jnp.einsum('eik,ekr->eir', couple, gathered, preferred_element_type=jnp.f...]
    gather x26 -> x0, local copies, waits for them, and re-layouts: 20.8 us -> none  [the longest x13 12.1 us: couple_apply(): jnp.take(extended, positions, axis=0).reshape(local_count, FACES * DOF, RHS)]
    ppermute x26 -> x42, waiting for transfers between devices: 17 us -> 35.5 us  [the longest x16 32 us: total(): lax.ppermute(value, AXES, [(d, d ^ step) for d in range(devices)])]
  transfers between devices with their start and end apart: 30 -> 42, of which waited for: 11 -> 27; matrix products, arithmetic and copies ran while one was open for 5% -> 0% of each run, Pallas kernels for 0% -> 0%
where the time goes in v1:
time: 213 us; the launch traced here: 212 us
  starting transfers between devices  114 us (54%)
  Pallas kernels  57.6 us (27%)
  waiting for transfers between devices  35.5 us (17%)
  local copies, waits for them, and re-layouts  3.89 us (2%)
    ppermute x16, starting transfers between devices, total(): lax.ppermute(value, AXES, [(d, d ^ step) for d in range(devices)])  57.2 us
    ppermute x13, starting transfers between devices, exchange(): from_chip = lax.ppermute(to_chip, AXES, chip_pairs)  47.8 us
    ppermute x16, waiting for transfers between devices, total(): lax.ppermute(value, AXES, [(d, d ^ step) for d in range(devices)])  32 us
    pallas_call x3, Pallas kernels, shards(): x, r, own, to_chip, to_link = update(lists, sums, r, b1, b2, b3, x)  29.7 us
    pallas_call x8, Pallas kernels, shards(): power(lists, positions, couple, own, *exchange(to_chip, to_link))  10.2 us
    pallas_call x1, Pallas kernels, shards(): x, r = finish(sums, r, b1, b2, b3, x)  8.96 us
    ppermute x13, starting transfers between devices, exchange(): from_link = lax.ppermute(to_link, AXES, link_pairs)  8.92 us
    pallas_call x4, Pallas kernels, shards(): gram(positions, couple, own, *exchange(to_chip, to_link), r, b1, b2)  6.77 us
  transfers between devices with their start and end apart: 42, of which 27 were waited for; matrix products, arithmetic and copies ran while one was open for 0% of the time, Pallas kernels for 0%

profile of v1, /device:TPU:0, one launch (start us, length us, event | category | flops | bytes accessed | tf_op | source)
XLA Modules:
  0.0 212.1 jit_solution(5045240269382454517)
XLA Ops:
  6.0 5.6 %collective-permute-start.2 = (bf16[4,64,32]{2,1,0:T(8,128)(2,1)S(1)}, bf16[4,64,32]{2,1,0:T(8,128)(2,1)S(1)}, u32[]{:S(2)}, u32[]{:S(2)}) collective-permute-start(bf16[4,64,32]{2,1,0:T(8,128)(2,1)S(1)} %get-tuple-element.70), channel_id=1, source_target_pairs={{0,1},{1,0},{2,3},{3,2},{4,5},{5,4},{6,7},{7,6},{8,9},{9,8},{10,11... | collective-permute-start | bytes 49160 | tf_op jit(solution)/shard_map/ppermute | solution.py:185
  13.8 6.1 %collective-permute-start.4 = (bf16[4,64,32]{2,1,0:T(8,128)(2,1)S(1)}, bf16[4,64,32]{2,1,0:T(8,128)(2,1)S(1)}, u32[]{:S(2)}, u32[]{:S(2)}) collective-permute-start(bf16[4,64,32]{2,1,0:T(8,128)(2,1)S(1)} %get-tuple-element.73), channel_id=1, source_target_pairs={{0,1},{1,0},{2,3},{3,2},{4,5},{5,4},{6,7},{7,6},{8,9},{9,8},{10,11... | collective-permute-start | bytes 49160 | tf_op jit(solution)/shard_map/ppermute | solution.py:185
  22.1 5.7 %collective-permute-start.6 = (bf16[4,64,32]{2,1,0:T(8,128)(2,1)S(1)}, bf16[4,64,32]{2,1,0:T(8,128)(2,1)S(1)}, u32[]{:S(2)}, u32[]{:S(2)}) collective-permute-start(bf16[4,64,32]{2,1,0:T(8,128)(2,1)S(1)} %get-tuple-element.76), channel_id=1, source_target_pairs={{0,1},{1,0},{2,3},{3,2},{4,5},{5,4},{6,7},{7,6},{8,9},{9,8},{10,11... | collective-permute-start | bytes 49160 | tf_op jit(solution)/shard_map/ppermute | solution.py:185
  30.4 5.7 %collective-permute-start.8 = (f32[128,128]{1,0:T(8,128)S(1)}, f32[128,128]{1,0:T(8,128)S(1)}, u32[]{:S(2)}, u32[]{:S(2)}) collective-permute-start(f32[128,128]{1,0:T(8,128)S(1)} %get-tuple-element.81), channel_id=1, source_target_pairs={{0,1},{1,0},{2,3},{3,2},{4,5},{5,4},{6,7},{7,6},{8,9},{9,8},{10,11... | collective-permute-start | bytes 196616 | tf_op jit(solution)/shard_map/ppermute | solution.py:191
  46.8 3.1 %collective-permute-start.11 = (f32[128,128]{1,0:T(8,128)S(1)}, f32[128,128]{1,0:T(8,128)S(1)}, u32[]{:S(2)}, u32[]{:S(2)}) collective-permute-start(f32[128,128]{1,0:T(8,128)S(1)} %add.55), channel_id=1, source_target_pairs={{0,8},{1,9},{2,10},{3,11},{4,12},{5,13},{6,14},{7,15},{8,0},{9,1},... | collective-permute-start | bytes 196616 | tf_op jit(solution)/shard_map/ppermute | solution.py:191
  52.2 9.9 %solve_update.3 = (f32[16,64,32]{2,1,0:T(8,128)S(1)}, f32[16,64,32]{2,1,0:T(8,128)S(1)}, bf16[16,64,32]{2,1,0:T(8,128)(2,1)S(1)}, bf16[4,64,32]{2,1,0:T(8,128)(2,1)S(1)}, bf16[4,64,32]{2,1,0:T(8,128)(2,1)S(1)}) custom-call(s32[2,4]{1,0:T(2,128)S(1)} %broadcast_select_fusion.lists, f32[128,128]{1,0:T(8,128)S(1)} %add.56.gram, ...), custom_call_target="tpu_custom_call" | custom-call | tf_op jit(solution)/shard_map/solve_update/pallas_call | solution.py:219
  64.7 4.9 %collective-permute-start.14 = (bf16[4,64,32]{2,1,0:T(8,128)(2,1)S(1)}, bf16[4,64,32]{2,1,0:T(8,128)(2,1)S(1)}, u32[]{:S(2)}, u32[]{:S(2)}) collective-permute-start(bf16[4,64,32]{2,1,0:T(8,128)(2,1)S(1)} %get-tuple-element.87), channel_id=1, source_target_pairs={{0,1},{1,0},{2,3},{3,2},{4,5},{5,4},{6,7},{7,6},{8,9},{9,8},{10,11... | collective-permute-start | bytes 49160 | tf_op jit(solution)/shard_map/ppermute | solution.py:185
  71.8 5.3 %collective-permute-start.16 = (bf16[4,64,32]{2,1,0:T(8,128)(2,1)S(1)}, bf16[4,64,32]{2,1,0:T(8,128)(2,1)S(1)}, u32[]{:S(2)}, u32[]{:S(2)}) collective-permute-start(bf16[4,64,32]{2,1,0:T(8,128)(2,1)S(1)} %get-tuple-element.90), channel_id=1, source_target_pairs={{0,1},{1,0},{2,3},{3,2},{4,5},{5,4},{6,7},{7,6},{8,9},{9,8},{10,11... | collective-permute-start | bytes 49160 | tf_op jit(solution)/shard_map/ppermute | solution.py:185
  79.7 5.7 %collective-permute-start.18 = (f32[128,128]{1,0:T(8,128)S(1)}, f32[128,128]{1,0:T(8,128)S(1)}, u32[]{:S(2)}, u32[]{:S(2)}) collective-permute-start(f32[128,128]{1,0:T(8,128)S(1)} %get-tuple-element.95), channel_id=1, source_target_pairs={{0,1},{1,0},{2,3},{3,2},{4,5},{5,4},{6,7},{7,6},{8,9},{9,8},{10,11... | collective-permute-start | bytes 196616 | tf_op jit(solution)/shard_map/ppermute | solution.py:191
  96.4 3.2 %collective-permute-start.21 = (f32[128,128]{1,0:T(8,128)S(1)}, f32[128,128]{1,0:T(8,128)S(1)}, u32[]{:S(2)}, u32[]{:S(2)}) collective-permute-start(f32[128,128]{1,0:T(8,128)S(1)} %add.59), channel_id=1, source_target_pairs={{0,8},{1,9},{2,10},{3,11},{4,12},{5,13},{6,14},{7,15},{8,0},{9,1},... | collective-permute-start | bytes 196616 | tf_op jit(solution)/shard_map/ppermute | solution.py:191
  101.9 9.9 %solve_update.4 = (f32[16,64,32]{2,1,0:T(8,128)S(1)}, f32[16,64,32]{2,1,0:T(8,128)S(1)}, bf16[16,64,32]{2,1,0:T(8,128)(2,1)S(1)}, bf16[4,64,32]{2,1,0:T(8,128)(2,1)S(1)}, bf16[4,64,32]{2,1,0:T(8,128)(2,1)S(1)}) custom-call(s32[2,4]{1,0:T(2,128)S(1)} %broadcast_select_fusion.lists, f32[128,128]{1,0:T(8,128)S(1)} %add.60.gram, ...), custom_call_target="tpu_custom_call" | custom-call | tf_op jit(solution)/shard_map/solve_update/pallas_call | solution.py:219
  114.4 4.9 %collective-permute-start.24 = (bf16[4,64,32]{2,1,0:T(8,128)(2,1)S(1)}, bf16[4,64,32]{2,1,0:T(8,128)(2,1)S(1)}, u32[]{:S(2)}, u32[]{:S(2)}) collective-permute-start(bf16[4,64,32]{2,1,0:T(8,128)(2,1)S(1)} %get-tuple-element.102), channel_id=1, source_target_pairs={{0,1},{1,0},{2,3},{3,2},{4,5},{5,4},{6,7},{7,6},{8,9},{9,8},{10,11... | collective-permute-start | bytes 49160 | tf_op jit(solution)/shard_map/ppermute | solution.py:185
  121.5 4.9 %collective-permute-start.26 = (bf16[4,64,32]{2,1,0:T(8,128)(2,1)S(1)}, bf16[4,64,32]{2,1,0:T(8,128)(2,1)S(1)}, u32[]{:S(2)}, u32[]{:S(2)}) collective-permute-start(bf16[4,64,32]{2,1,0:T(8,128)(2,1)S(1)} %get-tuple-element.105), channel_id=1, source_target_pairs={{0,1},{1,0},{2,3},{3,2},{4,5},{5,4},{6,7},{7,6},{8,9},{9,8},{10,11... | collective-permute-start | bytes 49160 | tf_op jit(solution)/shard_map/ppermute | solution.py:185
  129.0 5.7 %collective-permute-start.28 = (f32[128,128]{1,0:T(8,128)S(1)}, f32[128,128]{1,0:T(8,128)S(1)}, u32[]{:S(2)}, u32[]{:S(2)}) collective-permute-start(f32[128,128]{1,0:T(8,128)S(1)} %get-tuple-element.110), channel_id=1, source_target_pairs={{0,1},{1,0},{2,3},{3,2},{4,5},{5,4},{6,7},{7,6},{8,9},{9,8},{10,11... | collective-permute-start | bytes 196616 | tf_op jit(solution)/shard_map/ppermute | solution.py:191
  140.8 3.2 %collective-permute-start.30 = (f32[128,128]{1,0:T(8,128)S(1)}, f32[128,128]{1,0:T(8,128)S(1)}, u32[]{:S(2)}, u32[]{:S(2)}) collective-permute-start(f32[128,128]{1,0:T(8,128)S(1)} %add.62), channel_id=1, source_target_pairs={{0,4},{1,5},{2,6},{3,7},{4,0},{5,1},{6,2},{7,3},{8,12},{9,13},{10,... | collective-permute-start | bytes 196616 | tf_op jit(solution)/shard_map/ppermute | solution.py:191
  146.3 3.1 %collective-permute-start.31 = (f32[128,128]{1,0:T(8,128)S(1)}, f32[128,128]{1,0:T(8,128)S(1)}, u32[]{:S(2)}, u32[]{:S(2)}) collective-permute-start(f32[128,128]{1,0:T(8,128)S(1)} %add.63), channel_id=1, source_target_pairs={{0,8},{1,9},{2,10},{3,11},{4,12},{5,13},{6,14},{7,15},{8,0},{9,1},... | collective-permute-start | bytes 196616 | tf_op jit(solution)/shard_map/ppermute | solution.py:191
  151.7 9.9 %solve_update.5 = (f32[16,64,32]{2,1,0:T(8,128)S(1)}, f32[16,64,32]{2,1,0:T(8,128)S(1)}, bf16[16,64,32]{2,1,0:T(8,128)(2,1)S(1)}, bf16[4,64,32]{2,1,0:T(8,128)(2,1)S(1)}, bf16[4,64,32]{2,1,0:T(8,128)(2,1)S(1)}) custom-call(s32[2,4]{1,0:T(2,128)S(1)} %broadcast_select_fusion.lists, f32[128,128]{1,0:T(8,128)S(1)} %add.64.gram, ...), custom_call_target="tpu_custom_call" | custom-call | tf_op jit(solution)/shard_map/solve_update/pallas_call | solution.py:219
  164.1 4.9 %collective-permute-start.34 = (bf16[4,64,32]{2,1,0:T(8,128)(2,1)S(1)}, bf16[4,64,32]{2,1,0:T(8,128)(2,1)S(1)}, u32[]{:S(2)}, u32[]{:S(2)}) collective-permute-start(bf16[4,64,32]{2,1,0:T(8,128)(2,1)S(1)} %get-tuple-element.117), channel_id=1, source_target_pairs={{0,1},{1,0},{2,3},{3,2},{4,5},{5,4},{6,7},{7,6},{8,9},{9,8},{10,11... | collective-permute-start | bytes 49160 | tf_op jit(solution)/shard_map/ppermute | solution.py:185
  171.2 4.8 %collective-permute-start.36 = (bf16[4,64,32]{2,1,0:T(8,128)(2,1)S(1)}, bf16[4,64,32]{2,1,0:T(8,128)(2,1)S(1)}, u32[]{:S(2)}, u32[]{:S(2)}) collective-permute-start(bf16[4,64,32]{2,1,0:T(8,128)(2,1)S(1)} %get-tuple-element.120), channel_id=1, source_target_pairs={{0,1},{1,0},{2,3},{3,2},{4,5},{5,4},{6,7},{7,6},{8,9},{9,8},{10,11... | collective-permute-start | bytes 49160 | tf_op jit(solution)/shard_map/ppermute | solution.py:185
  178.6 5.7 %collective-permute-start.38 = (f32[128,128]{1,0:T(8,128)S(1)}, f32[128,128]{1,0:T(8,128)S(1)}, u32[]{:S(2)}, u32[]{:S(2)}) collective-permute-start(f32[128,128]{1,0:T(8,128)S(1)} %get-tuple-element.125), channel_id=1, source_target_pairs={{0,1},{1,0},{2,3},{3,2},{4,5},{5,4},{6,7},{7,6},{8,9},{9,8},{10,11... | collective-permute-start | bytes 196616 | tf_op jit(solution)/shard_map/ppermute | solution.py:191
  185.1 2.7 %collective-permute-start.39 = (f32[128,128]{1,0:T(8,128)S(1)}, f32[128,128]{1,0:T(8,128)S(1)}, u32[]{:S(2)}, u32[]{:S(2)}) collective-permute-start(f32[128,128]{1,0:T(8,128)S(1)} %add.65), channel_id=1, source_target_pairs={{0,2},{1,3},{2,0},{3,1},{4,6},{5,7},{6,4},{7,5},{8,10},{9,11},{10,... | collective-permute-start | bytes 196616 | tf_op jit(solution)/shard_map/ppermute | solution.py:191
  190.5 3.2 %collective-permute-start.40 = (f32[128,128]{1,0:T(8,128)S(1)}, f32[128,128]{1,0:T(8,128)S(1)}, u32[]{:S(2)}, u32[]{:S(2)}) collective-permute-start(f32[128,128]{1,0:T(8,128)S(1)} %add.66), channel_id=1, source_target_pairs={{0,4},{1,5},{2,6},{3,7},{4,0},{5,1},{6,2},{7,3},{8,12},{9,13},{10,... | collective-permute-start | bytes 196616 | tf_op jit(solution)/shard_map/ppermute | solution.py:191
  196.0 3.1 %collective-permute-start.41 = (f32[128,128]{1,0:T(8,128)S(1)}, f32[128,128]{1,0:T(8,128)S(1)}, u32[]{:S(2)}, u32[]{:S(2)}) collective-permute-start(f32[128,128]{1,0:T(8,128)S(1)} %add.67), channel_id=1, source_target_pairs={{0,8},{1,9},{2,10},{3,11},{4,12},{5,13},{6,14},{7,15},{8,0},{9,1},... | collective-permute-start | bytes 196616 | tf_op jit(solution)/shard_map/ppermute | solution.py:191
  201.4 9.0 %solve_finish.1 = (f32[16,64,32]{2,1,0:T(8,128)S(1)}, f32[16,64,32]{2,1,0:T(8,128)S(1)}) custom-call(f32[128,128]{1,0:T(8,128)S(1)} %add.68.gram, f32[16,64,32]{2,1,0:T(8,128)S(1)} %get-tuple-element.122.b0, f32[16,64,32]{2,1,0:T(8,128)S(1)} %get-tuple-element.123.b1, f32[16,64,32]{2,1,0:T(8,128)S(1)} %get-tuple-element.124.b2, ...), custom_call_target="tpu_custom_call" | custom-call | tf_op jit(solution)/shard_map/solve_finish/pallas_call | solution.py:221
  (111 shorter events, 81.0 us)
Async XLA Ops:
  6.0 6.5 %collective-permute-start.2 = (bf16[4,64,32]{2,1,0:T(8,128)(2,1)S(1)}, bf16[4,64,32]{2,1,0:T(8,128)(2,1)S(1)}, u32[]{:S(2)}, u32[]{:S(2)}) collective-permute-start(bf16[4,64,32]{2,1,0:T(8,128)(2,1)S(1)} %get-tuple-element.70), channel_id=1, source_target_pairs={{0,1},{1,0},{2,3},{3,2},{4,5},{5,4},{6,7},{7,6},{8,9},{9,8},{10,11... | collective-permute-start | bytes 49160 | tf_op jit(solution)/shard_map/ppermute | solution.py:185
  13.8 7.0 %collective-permute-start.4 = (bf16[4,64,32]{2,1,0:T(8,128)(2,1)S(1)}, bf16[4,64,32]{2,1,0:T(8,128)(2,1)S(1)}, u32[]{:S(2)}, u32[]{:S(2)}) collective-permute-start(bf16[4,64,32]{2,1,0:T(8,128)(2,1)S(1)} %get-tuple-element.73), channel_id=1, source_target_pairs={{0,1},{1,0},{2,3},{3,2},{4,5},{5,4},{6,7},{7,6},{8,9},{9,8},{10,11... | collective-permute-start | bytes 49160 | tf_op jit(solution)/shard_map/ppermute | solution.py:185
  22.1 6.6 %collective-permute-start.6 = (bf16[4,64,32]{2,1,0:T(8,128)(2,1)S(1)}, bf16[4,64,32]{2,1,0:T(8,128)(2,1)S(1)}, u32[]{:S(2)}, u32[]{:S(2)}) collective-permute-start(bf16[4,64,32]{2,1,0:T(8,128)(2,1)S(1)} %get-tuple-element.76), channel_id=1, source_target_pairs={{0,1},{1,0},{2,3},{3,2},{4,5},{5,4},{6,7},{7,6},{8,9},{9,8},{10,11... | collective-permute-start | bytes 49160 | tf_op jit(solution)/shard_map/ppermute | solution.py:185
  30.4 6.6 %collective-permute-start.8 = (f32[128,128]{1,0:T(8,128)S(1)}, f32[128,128]{1,0:T(8,128)S(1)}, u32[]{:S(2)}, u32[]{:S(2)}) collective-permute-start(f32[128,128]{1,0:T(8,128)S(1)} %get-tuple-element.81), channel_id=1, source_target_pairs={{0,1},{1,0},{2,3},{3,2},{4,5},{5,4},{6,7},{7,6},{8,9},{9,8},{10,11... | collective-permute-start | bytes 196616 | tf_op jit(solution)/shard_map/ppermute | solution.py:191
  36.9 5.2 %collective-permute-start.9 = (f32[128,128]{1,0:T(8,128)S(1)}, f32[128,128]{1,0:T(8,128)S(1)}, u32[]{:S(2)}, u32[]{:S(2)}) collective-permute-start(f32[128,128]{1,0:T(8,128)S(1)} %add.53), channel_id=1, source_target_pairs={{0,2},{1,3},{2,0},{3,1},{4,6},{5,7},{6,4},{7,5},{8,10},{9,11},{10,... | collective-permute-start | bytes 196616 | tf_op jit(solution)/shard_map/ppermute | solution.py:191
  46.8 5.4 %collective-permute-start.11 = (f32[128,128]{1,0:T(8,128)S(1)}, f32[128,128]{1,0:T(8,128)S(1)}, u32[]{:S(2)}, u32[]{:S(2)}) collective-permute-start(f32[128,128]{1,0:T(8,128)S(1)} %add.55), channel_id=1, source_target_pairs={{0,8},{1,9},{2,10},{3,11},{4,12},{5,13},{6,14},{7,15},{8,0},{9,1},... | collective-permute-start | bytes 196616 | tf_op jit(solution)/shard_map/ppermute | solution.py:191
  64.7 5.8 %collective-permute-start.14 = (bf16[4,64,32]{2,1,0:T(8,128)(2,1)S(1)}, bf16[4,64,32]{2,1,0:T(8,128)(2,1)S(1)}, u32[]{:S(2)}, u32[]{:S(2)}) collective-permute-start(bf16[4,64,32]{2,1,0:T(8,128)(2,1)S(1)} %get-tuple-element.87), channel_id=1, source_target_pairs={{0,1},{1,0},{2,3},{3,2},{4,5},{5,4},{6,7},{7,6},{8,9},{9,8},{10,11... | collective-permute-start | bytes 49160 | tf_op jit(solution)/shard_map/ppermute | solution.py:185
  71.8 6.2 %collective-permute-start.16 = (bf16[4,64,32]{2,1,0:T(8,128)(2,1)S(1)}, bf16[4,64,32]{2,1,0:T(8,128)(2,1)S(1)}, u32[]{:S(2)}, u32[]{:S(2)}) collective-permute-start(bf16[4,64,32]{2,1,0:T(8,128)(2,1)S(1)} %get-tuple-element.90), channel_id=1, source_target_pairs={{0,1},{1,0},{2,3},{3,2},{4,5},{5,4},{6,7},{7,6},{8,9},{9,8},{10,11... | collective-permute-start | bytes 49160 | tf_op jit(solution)/shard_map/ppermute | solution.py:185
  79.7 6.6 %collective-permute-start.18 = (f32[128,128]{1,0:T(8,128)S(1)}, f32[128,128]{1,0:T(8,128)S(1)}, u32[]{:S(2)}, u32[]{:S(2)}) collective-permute-start(f32[128,128]{1,0:T(8,128)S(1)} %get-tuple-element.95), channel_id=1, source_target_pairs={{0,1},{1,0},{2,3},{3,2},{4,5},{5,4},{6,7},{7,6},{8,9},{9,8},{10,11... | collective-permute-start | bytes 196616 | tf_op jit(solution)/shard_map/ppermute | solution.py:191
  86.3 5.2 %collective-permute-start.19 = (f32[128,128]{1,0:T(8,128)S(1)}, f32[128,128]{1,0:T(8,128)S(1)}, u32[]{:S(2)}, u32[]{:S(2)}) collective-permute-start(f32[128,128]{1,0:T(8,128)S(1)} %add.57), channel_id=1, source_target_pairs={{0,2},{1,3},{2,0},{3,1},{4,6},{5,7},{6,4},{7,5},{8,10},{9,11},{10,... | collective-permute-start | bytes 196616 | tf_op jit(solution)/shard_map/ppermute | solution.py:191
  91.5 4.9 %collective-permute-start.20 = (f32[128,128]{1,0:T(8,128)S(1)}, f32[128,128]{1,0:T(8,128)S(1)}, u32[]{:S(2)}, u32[]{:S(2)}) collective-permute-start(f32[128,128]{1,0:T(8,128)S(1)} %add.58), channel_id=1, source_target_pairs={{0,4},{1,5},{2,6},{3,7},{4,0},{5,1},{6,2},{7,3},{8,12},{9,13},{10,... | collective-permute-start | bytes 196616 | tf_op jit(solution)/shard_map/ppermute | solution.py:191
  96.4 5.5 %collective-permute-start.21 = (f32[128,128]{1,0:T(8,128)S(1)}, f32[128,128]{1,0:T(8,128)S(1)}, u32[]{:S(2)}, u32[]{:S(2)}) collective-permute-start(f32[128,128]{1,0:T(8,128)S(1)} %add.59), channel_id=1, source_target_pairs={{0,8},{1,9},{2,10},{3,11},{4,12},{5,13},{6,14},{7,15},{8,0},{9,1},... | collective-permute-start | bytes 196616 | tf_op jit(solution)/shard_map/ppermute | solution.py:191
  114.4 5.8 %collective-permute-start.24 = (bf16[4,64,32]{2,1,0:T(8,128)(2,1)S(1)}, bf16[4,64,32]{2,1,0:T(8,128)(2,1)S(1)}, u32[]{:S(2)}, u32[]{:S(2)}) collective-permute-start(bf16[4,64,32]{2,1,0:T(8,128)(2,1)S(1)} %get-tuple-element.102), channel_id=1, source_target_pairs={{0,1},{1,0},{2,3},{3,2},{4,5},{5,4},{6,7},{7,6},{8,9},{9,8},{10,11... | collective-permute-start | bytes 49160 | tf_op jit(solution)/shard_map/ppermute | solution.py:185
  121.5 5.8 %collective-permute-start.26 = (bf16[4,64,32]{2,1,0:T(8,128)(2,1)S(1)}, bf16[4,64,32]{2,1,0:T(8,128)(2,1)S(1)}, u32[]{:S(2)}, u32[]{:S(2)}) collective-permute-start(bf16[4,64,32]{2,1,0:T(8,128)(2,1)S(1)} %get-tuple-element.105), channel_id=1, source_target_pairs={{0,1},{1,0},{2,3},{3,2},{4,5},{5,4},{6,7},{7,6},{8,9},{9,8},{10,11... | collective-permute-start | bytes 49160 | tf_op jit(solution)/shard_map/ppermute | solution.py:185
  129.0 6.6 %collective-permute-start.28 = (f32[128,128]{1,0:T(8,128)S(1)}, f32[128,128]{1,0:T(8,128)S(1)}, u32[]{:S(2)}, u32[]{:S(2)}) collective-permute-start(f32[128,128]{1,0:T(8,128)S(1)} %get-tuple-element.110), channel_id=1, source_target_pairs={{0,1},{1,0},{2,3},{3,2},{4,5},{5,4},{6,7},{7,6},{8,9},{9,8},{10,11... | collective-permute-start | bytes 196616 | tf_op jit(solution)/shard_map/ppermute | solution.py:191
  135.6 5.2 %collective-permute-start.29 = (f32[128,128]{1,0:T(8,128)S(1)}, f32[128,128]{1,0:T(8,128)S(1)}, u32[]{:S(2)}, u32[]{:S(2)}) collective-permute-start(f32[128,128]{1,0:T(8,128)S(1)} %add.61), channel_id=1, source_target_pairs={{0,2},{1,3},{2,0},{3,1},{4,6},{5,7},{6,4},{7,5},{8,10},{9,11},{10,... | collective-permute-start | bytes 196616 | tf_op jit(solution)/shard_map/ppermute | solution.py:191
  140.8 5.4 %collective-permute-start.30 = (f32[128,128]{1,0:T(8,128)S(1)}, f32[128,128]{1,0:T(8,128)S(1)}, u32[]{:S(2)}, u32[]{:S(2)}) collective-permute-start(f32[128,128]{1,0:T(8,128)S(1)} %add.62), channel_id=1, source_target_pairs={{0,4},{1,5},{2,6},{3,7},{4,0},{5,1},{6,2},{7,3},{8,12},{9,13},{10,... | collective-permute-start | bytes 196616 | tf_op jit(solution)/shard_map/ppermute | solution.py:191
  146.3 5.4 %collective-permute-start.31 = (f32[128,128]{1,0:T(8,128)S(1)}, f32[128,128]{1,0:T(8,128)S(1)}, u32[]{:S(2)}, u32[]{:S(2)}) collective-permute-start(f32[128,128]{1,0:T(8,128)S(1)} %add.63), channel_id=1, source_target_pairs={{0,8},{1,9},{2,10},{3,11},{4,12},{5,13},{6,14},{7,15},{8,0},{9,1},... | collective-permute-start | bytes 196616 | tf_op jit(solution)/shard_map/ppermute | solution.py:191
  164.1 5.8 %collective-permute-start.34 = (bf16[4,64,32]{2,1,0:T(8,128)(2,1)S(1)}, bf16[4,64,32]{2,1,0:T(8,128)(2,1)S(1)}, u32[]{:S(2)}, u32[]{:S(2)}) collective-permute-start(bf16[4,64,32]{2,1,0:T(8,128)(2,1)S(1)} %get-tuple-element.117), channel_id=1, source_target_pairs={{0,1},{1,0},{2,3},{3,2},{4,5},{5,4},{6,7},{7,6},{8,9},{9,8},{10,11... | collective-permute-start | bytes 49160 | tf_op jit(solution)/shard_map/ppermute | solution.py:185
  171.2 5.7 %collective-permute-start.36 = (bf16[4,64,32]{2,1,0:T(8,128)(2,1)S(1)}, bf16[4,64,32]{2,1,0:T(8,128)(2,1)S(1)}, u32[]{:S(2)}, u32[]{:S(2)}) collective-permute-start(bf16[4,64,32]{2,1,0:T(8,128)(2,1)S(1)} %get-tuple-element.120), channel_id=1, source_target_pairs={{0,1},{1,0},{2,3},{3,2},{4,5},{5,4},{6,7},{7,6},{8,9},{9,8},{10,11... | collective-permute-start | bytes 49160 | tf_op jit(solution)/shard_map/ppermute | solution.py:185
  178.6 6.6 %collective-permute-start.38 = (f32[128,128]{1,0:T(8,128)S(1)}, f32[128,128]{1,0:T(8,128)S(1)}, u32[]{:S(2)}, u32[]{:S(2)}) collective-permute-start(f32[128,128]{1,0:T(8,128)S(1)} %get-tuple-element.125), channel_id=1, source_target_pairs={{0,1},{1,0},{2,3},{3,2},{4,5},{5,4},{6,7},{7,6},{8,9},{9,8},{10,11... | collective-permute-start | bytes 196616 | tf_op jit(solution)/shard_map/ppermute | solution.py:191
  185.1 5.3 %collective-permute-start.39 = (f32[128,128]{1,0:T(8,128)S(1)}, f32[128,128]{1,0:T(8,128)S(1)}, u32[]{:S(2)}, u32[]{:S(2)}) collective-permute-start(f32[128,128]{1,0:T(8,128)S(1)} %add.65), channel_id=1, source_target_pairs={{0,2},{1,3},{2,0},{3,1},{4,6},{5,7},{6,4},{7,5},{8,10},{9,11},{10,... | collective-permute-start | bytes 196616 | tf_op jit(solution)/shard_map/ppermute | solution.py:191
  190.5 5.5 %collective-permute-start.40 = (f32[128,128]{1,0:T(8,128)S(1)}, f32[128,128]{1,0:T(8,128)S(1)}, u32[]{:S(2)}, u32[]{:S(2)}) collective-permute-start(f32[128,128]{1,0:T(8,128)S(1)} %add.66), channel_id=1, source_target_pairs={{0,4},{1,5},{2,6},{3,7},{4,0},{5,1},{6,2},{7,3},{8,12},{9,13},{10,... | collective-permute-start | bytes 196616 | tf_op jit(solution)/shard_map/ppermute | solution.py:191
  196.0 5.4 %collective-permute-start.41 = (f32[128,128]{1,0:T(8,128)S(1)}, f32[128,128]{1,0:T(8,128)S(1)}, u32[]{:S(2)}, u32[]{:S(2)}) collective-permute-start(f32[128,128]{1,0:T(8,128)S(1)} %add.67), channel_id=1, source_target_pairs={{0,8},{1,9},{2,10},{3,11},{4,12},{5,13},{6,14},{7,15},{8,0},{9,1},... | collective-permute-start | bytes 196616 | tf_op jit(solution)/shard_map/ppermute | solution.py:191
  (22 other events, 30.7 us)

commit v2 on v1

--- a/solution.py
+++ b/solution.py
@@ -94,16 +94,30 @@
 
 
 def eliminate(gram):
-    size = SSTEP * RHS
-    groups = [gram[8 * g : 8 * g + 8, :] for g in range(size // 8)]
-    row_ids = lax.broadcasted_iota(jnp.int32, groups[0].shape, 0)
-    for j in range(size):
-        home, place = divmod(j, 8)
-        row = groups[home][place : place + 1, :]
-        scaled = row / row[:, j : j + 1]
-        for g in range(size // 8):
-            updated = groups[g] - groups[g][:, j : j + 1] * scaled
-            groups[g] = jnp.where(row_ids == place, scaled, updated) if g == home else updated
+    count = SSTEP * RHS // 8
+    groups = [gram[8 * g : 8 * g + 8, :] for g in range(count)]
+    shape = groups[0].shape
+    row_ids = lax.broadcasted_iota(jnp.int32, shape, 0)
+    for home in range(count):
+        columns = [
+            [jnp.broadcast_to(group[:, 8 * home + m : 8 * home + m + 1], shape) for m in range(8)]
+            for group in groups
+        ]
+        own = list(columns[home])
+        panel = groups[home]
+        for m in range(8):
+            inverse = 1.0 / own[m][m : m + 1, :]
+            scaled = panel[m : m + 1, :] * inverse
+            panel = jnp.where(row_ids == m, scaled, panel - own[m] * scaled)
+            for k in range(m + 1, 8):
+                scaled = own[k][m : m + 1, :] * inverse
+                own[k] = jnp.where(row_ids == m, scaled, own[k] - own[m] * scaled)
+        for g in range(count):
+            if g == home:
+                groups[g] = panel
+                continue
+            for m in range(8):
+                groups[g] = groups[g] - columns[g][m] * panel[m : m + 1, :]
     return jnp.concatenate(groups, axis=0)
 
 

time: 213 us -> 190 us (0.89)
  Pallas kernels: 57.6 us -> 35.4 us
    pallas_call x3, Pallas kernels: 29.7 us -> 12.9 us  [shards(): x, r, own, to_chip, to_link = update(lists, sums, r, b1, b2, b3, x)]
    pallas_call x1, Pallas kernels: 8.96 us -> 3.51 us  [shards(): x, r = finish(sums, r, b1, b2, b3, x)]
where the time goes in v2:
time: 190 us
  starting transfers between devices  114 us (60%)
  waiting for transfers between devices  35.5 us (19%)
  Pallas kernels  35.4 us (19%)
  local copies, waits for them, and re-layouts  3.89 us (2%)
    ppermute x16, starting transfers between devices, total(): lax.ppermute(value, AXES, [(d, d ^ step) for d in range(devices)])  57.2 us
    ppermute x13, starting transfers between devices, exchange(): from_chip = lax.ppermute(to_chip, AXES, chip_pairs)  47.8 us
    ppermute x16, waiting for transfers between devices, total(): lax.ppermute(value, AXES, [(d, d ^ step) for d in range(devices)])  32 us
    pallas_call x3, Pallas kernels, shards(): x, r, own, to_chip, to_link = update(lists, sums, r, b1, b2, b3, x)  12.9 us
    pallas_call x8, Pallas kernels, shards(): power(lists, positions, couple, own, *exchange(to_chip, to_link))  10.2 us
    ppermute x13, starting transfers between devices, exchange(): from_link = lax.ppermute(to_link, AXES, link_pairs)  8.92 us
    pallas_call x4, Pallas kernels, shards(): gram(positions, couple, own, *exchange(to_chip, to_link), r, b1, b2)  6.77 us
  transfers between devices with their start and end apart: 42, of which 27 were waited for; matrix products, arithmetic and copies ran while one was open for 0% of the time, Pallas kernels for 0%

profile of v2, /device:TPU:0, one launch (start us, length us, event | category | flops | bytes accessed | tf_op | source)
XLA Modules:
  0.0 189.9 jit_solution(15686888200279161415)
XLA Ops:
  6.0 5.6 %collective-permute-start.2 = (bf16[4,64,32]{2,1,0:T(8,128)(2,1)S(1)}, bf16[4,64,32]{2,1,0:T(8,128)(2,1)S(1)}, u32[]{:S(2)}, u32[]{:S(2)}) collective-permute-start(bf16[4,64,32]{2,1,0:T(8,128)(2,1)S(1)} %get-tuple-element.70), channel_id=1, source_target_pairs={{0,1},{1,0},{2,3},{3,2},{4,5},{5,4},{6,7},{7,6},{8,9},{9,8},{10,11... | collective-permute-start | bytes 49160 | tf_op jit(solution)/shard_map/ppermute | solution.py:199
  13.8 6.1 %collective-permute-start.4 = (bf16[4,64,32]{2,1,0:T(8,128)(2,1)S(1)}, bf16[4,64,32]{2,1,0:T(8,128)(2,1)S(1)}, u32[]{:S(2)}, u32[]{:S(2)}) collective-permute-start(bf16[4,64,32]{2,1,0:T(8,128)(2,1)S(1)} %get-tuple-element.73), channel_id=1, source_target_pairs={{0,1},{1,0},{2,3},{3,2},{4,5},{5,4},{6,7},{7,6},{8,9},{9,8},{10,11... | collective-permute-start | bytes 49160 | tf_op jit(solution)/shard_map/ppermute | solution.py:199
  22.1 5.7 %collective-permute-start.6 = (bf16[4,64,32]{2,1,0:T(8,128)(2,1)S(1)}, bf16[4,64,32]{2,1,0:T(8,128)(2,1)S(1)}, u32[]{:S(2)}, u32[]{:S(2)}) collective-permute-start(bf16[4,64,32]{2,1,0:T(8,128)(2,1)S(1)} %get-tuple-element.76), channel_id=1, source_target_pairs={{0,1},{1,0},{2,3},{3,2},{4,5},{5,4},{6,7},{7,6},{8,9},{9,8},{10,11... | collective-permute-start | bytes 49160 | tf_op jit(solution)/shard_map/ppermute | solution.py:199
  30.4 5.7 %collective-permute-start.8 = (f32[128,128]{1,0:T(8,128)S(1)}, f32[128,128]{1,0:T(8,128)S(1)}, u32[]{:S(2)}, u32[]{:S(2)}) collective-permute-start(f32[128,128]{1,0:T(8,128)S(1)} %get-tuple-element.81), channel_id=1, source_target_pairs={{0,1},{1,0},{2,3},{3,2},{4,5},{5,4},{6,7},{7,6},{8,9},{9,8},{10,11... | collective-permute-start | bytes 196616 | tf_op jit(solution)/shard_map/ppermute | solution.py:205
  46.8 3.1 %collective-permute-start.11 = (f32[128,128]{1,0:T(8,128)S(1)}, f32[128,128]{1,0:T(8,128)S(1)}, u32[]{:S(2)}, u32[]{:S(2)}) collective-permute-start(f32[128,128]{1,0:T(8,128)S(1)} %add.55), channel_id=1, source_target_pairs={{0,8},{1,9},{2,10},{3,11},{4,12},{5,13},{6,14},{7,15},{8,0},{9,1},... | collective-permute-start | bytes 196616 | tf_op jit(solution)/shard_map/ppermute | solution.py:205
  52.2 4.3 %solve_update.3 = (f32[16,64,32]{2,1,0:T(8,128)S(1)}, f32[16,64,32]{2,1,0:T(8,128)S(1)}, bf16[16,64,32]{2,1,0:T(8,128)(2,1)S(1)}, bf16[4,64,32]{2,1,0:T(8,128)(2,1)S(1)}, bf16[4,64,32]{2,1,0:T(8,128)(2,1)S(1)}) custom-call(s32[2,4]{1,0:T(2,128)S(1)} %broadcast_select_fusion.lists, f32[128,128]{1,0:T(8,128)S(1)} %add.56.gram, ...), custom_call_target="tpu_custom_call" | custom-call | tf_op jit(solution)/shard_map/solve_update/pallas_call | solution.py:233
  59.1 4.9 %collective-permute-start.14 = (bf16[4,64,32]{2,1,0:T(8,128)(2,1)S(1)}, bf16[4,64,32]{2,1,0:T(8,128)(2,1)S(1)}, u32[]{:S(2)}, u32[]{:S(2)}) collective-permute-start(bf16[4,64,32]{2,1,0:T(8,128)(2,1)S(1)} %get-tuple-element.87), channel_id=1, source_target_pairs={{0,1},{1,0},{2,3},{3,2},{4,5},{5,4},{6,7},{7,6},{8,9},{9,8},{10,11... | collective-permute-start | bytes 49160 | tf_op jit(solution)/shard_map/ppermute | solution.py:199
  66.2 5.3 %collective-permute-start.16 = (bf16[4,64,32]{2,1,0:T(8,128)(2,1)S(1)}, bf16[4,64,32]{2,1,0:T(8,128)(2,1)S(1)}, u32[]{:S(2)}, u32[]{:S(2)}) collective-permute-start(bf16[4,64,32]{2,1,0:T(8,128)(2,1)S(1)} %get-tuple-element.90), channel_id=1, source_target_pairs={{0,1},{1,0},{2,3},{3,2},{4,5},{5,4},{6,7},{7,6},{8,9},{9,8},{10,11... | collective-permute-start | bytes 49160 | tf_op jit(solution)/shard_map/ppermute | solution.py:199
  74.1 5.7 %collective-permute-start.18 = (f32[128,128]{1,0:T(8,128)S(1)}, f32[128,128]{1,0:T(8,128)S(1)}, u32[]{:S(2)}, u32[]{:S(2)}) collective-permute-start(f32[128,128]{1,0:T(8,128)S(1)} %get-tuple-element.95), channel_id=1, source_target_pairs={{0,1},{1,0},{2,3},{3,2},{4,5},{5,4},{6,7},{7,6},{8,9},{9,8},{10,11... | collective-permute-start | bytes 196616 | tf_op jit(solution)/shard_map/ppermute | solution.py:205
  90.8 3.3 %collective-permute-start.21 = (f32[128,128]{1,0:T(8,128)S(1)}, f32[128,128]{1,0:T(8,128)S(1)}, u32[]{:S(2)}, u32[]{:S(2)}) collective-permute-start(f32[128,128]{1,0:T(8,128)S(1)} %add.59), channel_id=1, source_target_pairs={{0,8},{1,9},{2,10},{3,11},{4,12},{5,13},{6,14},{7,15},{8,0},{9,1},... | collective-permute-start | bytes 196616 | tf_op jit(solution)/shard_map/ppermute | solution.py:205
  96.3 4.3 %solve_update.4 = (f32[16,64,32]{2,1,0:T(8,128)S(1)}, f32[16,64,32]{2,1,0:T(8,128)S(1)}, bf16[16,64,32]{2,1,0:T(8,128)(2,1)S(1)}, bf16[4,64,32]{2,1,0:T(8,128)(2,1)S(1)}, bf16[4,64,32]{2,1,0:T(8,128)(2,1)S(1)}) custom-call(s32[2,4]{1,0:T(2,128)S(1)} %broadcast_select_fusion.lists, f32[128,128]{1,0:T(8,128)S(1)} %add.60.gram, ...), custom_call_target="tpu_custom_call" | custom-call | tf_op jit(solution)/shard_map/solve_update/pallas_call | solution.py:233
  103.3 4.9 %collective-permute-start.24 = (bf16[4,64,32]{2,1,0:T(8,128)(2,1)S(1)}, bf16[4,64,32]{2,1,0:T(8,128)(2,1)S(1)}, u32[]{:S(2)}, u32[]{:S(2)}) collective-permute-start(bf16[4,64,32]{2,1,0:T(8,128)(2,1)S(1)} %get-tuple-element.102), channel_id=1, source_target_pairs={{0,1},{1,0},{2,3},{3,2},{4,5},{5,4},{6,7},{7,6},{8,9},{9,8},{10,11... | collective-permute-start | bytes 49160 | tf_op jit(solution)/shard_map/ppermute | solution.py:199
  110.3 4.9 %collective-permute-start.26 = (bf16[4,64,32]{2,1,0:T(8,128)(2,1)S(1)}, bf16[4,64,32]{2,1,0:T(8,128)(2,1)S(1)}, u32[]{:S(2)}, u32[]{:S(2)}) collective-permute-start(bf16[4,64,32]{2,1,0:T(8,128)(2,1)S(1)} %get-tuple-element.105), channel_id=1, source_target_pairs={{0,1},{1,0},{2,3},{3,2},{4,5},{5,4},{6,7},{7,6},{8,9},{9,8},{10,11... | collective-permute-start | bytes 49160 | tf_op jit(solution)/shard_map/ppermute | solution.py:199
  117.9 5.7 %collective-permute-start.28 = (f32[128,128]{1,0:T(8,128)S(1)}, f32[128,128]{1,0:T(8,128)S(1)}, u32[]{:S(2)}, u32[]{:S(2)}) collective-permute-start(f32[128,128]{1,0:T(8,128)S(1)} %get-tuple-element.110), channel_id=1, source_target_pairs={{0,1},{1,0},{2,3},{3,2},{4,5},{5,4},{6,7},{7,6},{8,9},{9,8},{10,11... | collective-permute-start | bytes 196616 | tf_op jit(solution)/shard_map/ppermute | solution.py:205
  129.7 3.2 %collective-permute-start.30 = (f32[128,128]{1,0:T(8,128)S(1)}, f32[128,128]{1,0:T(8,128)S(1)}, u32[]{:S(2)}, u32[]{:S(2)}) collective-permute-start(f32[128,128]{1,0:T(8,128)S(1)} %add.62), channel_id=1, source_target_pairs={{0,4},{1,5},{2,6},{3,7},{4,0},{5,1},{6,2},{7,3},{8,12},{9,13},{10,... | collective-permute-start | bytes 196616 | tf_op jit(solution)/shard_map/ppermute | solution.py:205
  135.1 3.1 %collective-permute-start.31 = (f32[128,128]{1,0:T(8,128)S(1)}, f32[128,128]{1,0:T(8,128)S(1)}, u32[]{:S(2)}, u32[]{:S(2)}) collective-permute-start(f32[128,128]{1,0:T(8,128)S(1)} %add.63), channel_id=1, source_target_pairs={{0,8},{1,9},{2,10},{3,11},{4,12},{5,13},{6,14},{7,15},{8,0},{9,1},... | collective-permute-start | bytes 196616 | tf_op jit(solution)/shard_map/ppermute | solution.py:205
  140.5 4.3 %solve_update.5 = (f32[16,64,32]{2,1,0:T(8,128)S(1)}, f32[16,64,32]{2,1,0:T(8,128)S(1)}, bf16[16,64,32]{2,1,0:T(8,128)(2,1)S(1)}, bf16[4,64,32]{2,1,0:T(8,128)(2,1)S(1)}, bf16[4,64,32]{2,1,0:T(8,128)(2,1)S(1)}) custom-call(s32[2,4]{1,0:T(2,128)S(1)} %broadcast_select_fusion.lists, f32[128,128]{1,0:T(8,128)S(1)} %add.64.gram, ...), custom_call_target="tpu_custom_call" | custom-call | tf_op jit(solution)/shard_map/solve_update/pallas_call | solution.py:233
  147.4 4.9 %collective-permute-start.34 = (bf16[4,64,32]{2,1,0:T(8,128)(2,1)S(1)}, bf16[4,64,32]{2,1,0:T(8,128)(2,1)S(1)}, u32[]{:S(2)}, u32[]{:S(2)}) collective-permute-start(bf16[4,64,32]{2,1,0:T(8,128)(2,1)S(1)} %get-tuple-element.117), channel_id=1, source_target_pairs={{0,1},{1,0},{2,3},{3,2},{4,5},{5,4},{6,7},{7,6},{8,9},{9,8},{10,11... | collective-permute-start | bytes 49160 | tf_op jit(solution)/shard_map/ppermute | solution.py:199
  154.5 4.8 %collective-permute-start.36 = (bf16[4,64,32]{2,1,0:T(8,128)(2,1)S(1)}, bf16[4,64,32]{2,1,0:T(8,128)(2,1)S(1)}, u32[]{:S(2)}, u32[]{:S(2)}) collective-permute-start(bf16[4,64,32]{2,1,0:T(8,128)(2,1)S(1)} %get-tuple-element.120), channel_id=1, source_target_pairs={{0,1},{1,0},{2,3},{3,2},{4,5},{5,4},{6,7},{7,6},{8,9},{9,8},{10,11... | collective-permute-start | bytes 49160 | tf_op jit(solution)/shard_map/ppermute | solution.py:199
  161.8 5.7 %collective-permute-start.38 = (f32[128,128]{1,0:T(8,128)S(1)}, f32[128,128]{1,0:T(8,128)S(1)}, u32[]{:S(2)}, u32[]{:S(2)}) collective-permute-start(f32[128,128]{1,0:T(8,128)S(1)} %get-tuple-element.125), channel_id=1, source_target_pairs={{0,1},{1,0},{2,3},{3,2},{4,5},{5,4},{6,7},{7,6},{8,9},{9,8},{10,11... | collective-permute-start | bytes 196616 | tf_op jit(solution)/shard_map/ppermute | solution.py:205
  168.4 2.7 %collective-permute-start.39 = (f32[128,128]{1,0:T(8,128)S(1)}, f32[128,128]{1,0:T(8,128)S(1)}, u32[]{:S(2)}, u32[]{:S(2)}) collective-permute-start(f32[128,128]{1,0:T(8,128)S(1)} %add.65), channel_id=1, source_target_pairs={{0,2},{1,3},{2,0},{3,1},{4,6},{5,7},{6,4},{7,5},{8,10},{9,11},{10,... | collective-permute-start | bytes 196616 | tf_op jit(solution)/shard_map/ppermute | solution.py:205
  173.7 3.2 %collective-permute-start.40 = (f32[128,128]{1,0:T(8,128)S(1)}, f32[128,128]{1,0:T(8,128)S(1)}, u32[]{:S(2)}, u32[]{:S(2)}) collective-permute-start(f32[128,128]{1,0:T(8,128)S(1)} %add.66), channel_id=1, source_target_pairs={{0,4},{1,5},{2,6},{3,7},{4,0},{5,1},{6,2},{7,3},{8,12},{9,13},{10,... | collective-permute-start | bytes 196616 | tf_op jit(solution)/shard_map/ppermute | solution.py:205
  179.2 3.1 %collective-permute-start.41 = (f32[128,128]{1,0:T(8,128)S(1)}, f32[128,128]{1,0:T(8,128)S(1)}, u32[]{:S(2)}, u32[]{:S(2)}) collective-permute-start(f32[128,128]{1,0:T(8,128)S(1)} %add.67), channel_id=1, source_target_pairs={{0,8},{1,9},{2,10},{3,11},{4,12},{5,13},{6,14},{7,15},{8,0},{9,1},... | collective-permute-start | bytes 196616 | tf_op jit(solution)/shard_map/ppermute | solution.py:205
  184.6 3.5 %solve_finish.1 = (f32[16,64,32]{2,1,0:T(8,128)S(1)}, f32[16,64,32]{2,1,0:T(8,128)S(1)}) custom-call(f32[128,128]{1,0:T(8,128)S(1)} %add.68.gram, f32[16,64,32]{2,1,0:T(8,128)S(1)} %get-tuple-element.122.b0, f32[16,64,32]{2,1,0:T(8,128)S(1)} %get-tuple-element.123.b1, f32[16,64,32]{2,1,0:T(8,128)S(1)} %get-tuple-element.124.b2, ...), custom_call_target="tpu_custom_call" | custom-call | tf_op jit(solution)/shard_map/solve_finish/pallas_call | solution.py:235
  (111 shorter events, 81.0 us)
Async XLA Ops:
  6.0 6.5 %collective-permute-start.2 = (bf16[4,64,32]{2,1,0:T(8,128)(2,1)S(1)}, bf16[4,64,32]{2,1,0:T(8,128)(2,1)S(1)}, u32[]{:S(2)}, u32[]{:S(2)}) collective-permute-start(bf16[4,64,32]{2,1,0:T(8,128)(2,1)S(1)} %get-tuple-element.70), channel_id=1, source_target_pairs={{0,1},{1,0},{2,3},{3,2},{4,5},{5,4},{6,7},{7,6},{8,9},{9,8},{10,11... | collective-permute-start | bytes 49160 | tf_op jit(solution)/shard_map/ppermute | solution.py:199
  13.8 7.0 %collective-permute-start.4 = (bf16[4,64,32]{2,1,0:T(8,128)(2,1)S(1)}, bf16[4,64,32]{2,1,0:T(8,128)(2,1)S(1)}, u32[]{:S(2)}, u32[]{:S(2)}) collective-permute-start(bf16[4,64,32]{2,1,0:T(8,128)(2,1)S(1)} %get-tuple-element.73), channel_id=1, source_target_pairs={{0,1},{1,0},{2,3},{3,2},{4,5},{5,4},{6,7},{7,6},{8,9},{9,8},{10,11... | collective-permute-start | bytes 49160 | tf_op jit(solution)/shard_map/ppermute | solution.py:199
  22.1 6.6 %collective-permute-start.6 = (bf16[4,64,32]{2,1,0:T(8,128)(2,1)S(1)}, bf16[4,64,32]{2,1,0:T(8,128)(2,1)S(1)}, u32[]{:S(2)}, u32[]{:S(2)}) collective-permute-start(bf16[4,64,32]{2,1,0:T(8,128)(2,1)S(1)} %get-tuple-element.76), channel_id=1, source_target_pairs={{0,1},{1,0},{2,3},{3,2},{4,5},{5,4},{6,7},{7,6},{8,9},{9,8},{10,11... | collective-permute-start | bytes 49160 | tf_op jit(solution)/shard_map/ppermute | solution.py:199
  30.4 6.6 %collective-permute-start.8 = (f32[128,128]{1,0:T(8,128)S(1)}, f32[128,128]{1,0:T(8,128)S(1)}, u32[]{:S(2)}, u32[]{:S(2)}) collective-permute-start(f32[128,128]{1,0:T(8,128)S(1)} %get-tuple-element.81), channel_id=1, source_target_pairs={{0,1},{1,0},{2,3},{3,2},{4,5},{5,4},{6,7},{7,6},{8,9},{9,8},{10,11... | collective-permute-start | bytes 196616 | tf_op jit(solution)/shard_map/ppermute | solution.py:205
  36.9 5.2 %collective-permute-start.9 = (f32[128,128]{1,0:T(8,128)S(1)}, f32[128,128]{1,0:T(8,128)S(1)}, u32[]{:S(2)}, u32[]{:S(2)}) collective-permute-start(f32[128,128]{1,0:T(8,128)S(1)} %add.53), channel_id=1, source_target_pairs={{0,2},{1,3},{2,0},{3,1},{4,6},{5,7},{6,4},{7,5},{8,10},{9,11},{10,... | collective-permute-start | bytes 196616 | tf_op jit(solution)/shard_map/ppermute | solution.py:205
  46.8 5.4 %collective-permute-start.11 = (f32[128,128]{1,0:T(8,128)S(1)}, f32[128,128]{1,0:T(8,128)S(1)}, u32[]{:S(2)}, u32[]{:S(2)}) collective-permute-start(f32[128,128]{1,0:T(8,128)S(1)} %add.55), channel_id=1, source_target_pairs={{0,8},{1,9},{2,10},{3,11},{4,12},{5,13},{6,14},{7,15},{8,0},{9,1},... | collective-permute-start | bytes 196616 | tf_op jit(solution)/shard_map/ppermute | solution.py:205
  59.1 5.8 %collective-permute-start.14 = (bf16[4,64,32]{2,1,0:T(8,128)(2,1)S(1)}, bf16[4,64,32]{2,1,0:T(8,128)(2,1)S(1)}, u32[]{:S(2)}, u32[]{:S(2)}) collective-permute-start(bf16[4,64,32]{2,1,0:T(8,128)(2,1)S(1)} %get-tuple-element.87), channel_id=1, source_target_pairs={{0,1},{1,0},{2,3},{3,2},{4,5},{5,4},{6,7},{7,6},{8,9},{9,8},{10,11... | collective-permute-start | bytes 49160 | tf_op jit(solution)/shard_map/ppermute | solution.py:199
  66.2 6.2 %collective-permute-start.16 = (bf16[4,64,32]{2,1,0:T(8,128)(2,1)S(1)}, bf16[4,64,32]{2,1,0:T(8,128)(2,1)S(1)}, u32[]{:S(2)}, u32[]{:S(2)}) collective-permute-start(bf16[4,64,32]{2,1,0:T(8,128)(2,1)S(1)} %get-tuple-element.90), channel_id=1, source_target_pairs={{0,1},{1,0},{2,3},{3,2},{4,5},{5,4},{6,7},{7,6},{8,9},{9,8},{10,11... | collective-permute-start | bytes 49160 | tf_op jit(solution)/shard_map/ppermute | solution.py:199
  74.1 6.6 %collective-permute-start.18 = (f32[128,128]{1,0:T(8,128)S(1)}, f32[128,128]{1,0:T(8,128)S(1)}, u32[]{:S(2)}, u32[]{:S(2)}) collective-permute-start(f32[128,128]{1,0:T(8,128)S(1)} %get-tuple-element.95), channel_id=1, source_target_pairs={{0,1},{1,0},{2,3},{3,2},{4,5},{5,4},{6,7},{7,6},{8,9},{9,8},{10,11... | collective-permute-start | bytes 196616 | tf_op jit(solution)/shard_map/ppermute | solution.py:205
  80.7 5.2 %collective-permute-start.19 = (f32[128,128]{1,0:T(8,128)S(1)}, f32[128,128]{1,0:T(8,128)S(1)}, u32[]{:S(2)}, u32[]{:S(2)}) collective-permute-start(f32[128,128]{1,0:T(8,128)S(1)} %add.57), channel_id=1, source_target_pairs={{0,2},{1,3},{2,0},{3,1},{4,6},{5,7},{6,4},{7,5},{8,10},{9,11},{10,... | collective-permute-start | bytes 196616 | tf_op jit(solution)/shard_map/ppermute | solution.py:205
  85.9 4.9 %collective-permute-start.20 = (f32[128,128]{1,0:T(8,128)S(1)}, f32[128,128]{1,0:T(8,128)S(1)}, u32[]{:S(2)}, u32[]{:S(2)}) collective-permute-start(f32[128,128]{1,0:T(8,128)S(1)} %add.58), channel_id=1, source_target_pairs={{0,4},{1,5},{2,6},{3,7},{4,0},{5,1},{6,2},{7,3},{8,12},{9,13},{10,... | collective-permute-start | bytes 196616 | tf_op jit(solution)/shard_map/ppermute | solution.py:205
  90.8 5.5 %collective-permute-start.21 = (f32[128,128]{1,0:T(8,128)S(1)}, f32[128,128]{1,0:T(8,128)S(1)}, u32[]{:S(2)}, u32[]{:S(2)}) collective-permute-start(f32[128,128]{1,0:T(8,128)S(1)} %add.59), channel_id=1, source_target_pairs={{0,8},{1,9},{2,10},{3,11},{4,12},{5,13},{6,14},{7,15},{8,0},{9,1},... | collective-permute-start | bytes 196616 | tf_op jit(solution)/shard_map/ppermute | solution.py:205
  103.3 5.8 %collective-permute-start.24 = (bf16[4,64,32]{2,1,0:T(8,128)(2,1)S(1)}, bf16[4,64,32]{2,1,0:T(8,128)(2,1)S(1)}, u32[]{:S(2)}, u32[]{:S(2)}) collective-permute-start(bf16[4,64,32]{2,1,0:T(8,128)(2,1)S(1)} %get-tuple-element.102), channel_id=1, source_target_pairs={{0,1},{1,0},{2,3},{3,2},{4,5},{5,4},{6,7},{7,6},{8,9},{9,8},{10,11... | collective-permute-start | bytes 49160 | tf_op jit(solution)/shard_map/ppermute | solution.py:199
  110.3 5.8 %collective-permute-start.26 = (bf16[4,64,32]{2,1,0:T(8,128)(2,1)S(1)}, bf16[4,64,32]{2,1,0:T(8,128)(2,1)S(1)}, u32[]{:S(2)}, u32[]{:S(2)}) collective-permute-start(bf16[4,64,32]{2,1,0:T(8,128)(2,1)S(1)} %get-tuple-element.105), channel_id=1, source_target_pairs={{0,1},{1,0},{2,3},{3,2},{4,5},{5,4},{6,7},{7,6},{8,9},{9,8},{10,11... | collective-permute-start | bytes 49160 | tf_op jit(solution)/shard_map/ppermute | solution.py:199
  117.9 6.6 %collective-permute-start.28 = (f32[128,128]{1,0:T(8,128)S(1)}, f32[128,128]{1,0:T(8,128)S(1)}, u32[]{:S(2)}, u32[]{:S(2)}) collective-permute-start(f32[128,128]{1,0:T(8,128)S(1)} %get-tuple-element.110), channel_id=1, source_target_pairs={{0,1},{1,0},{2,3},{3,2},{4,5},{5,4},{6,7},{7,6},{8,9},{9,8},{10,11... | collective-permute-start | bytes 196616 | tf_op jit(solution)/shard_map/ppermute | solution.py:205
  124.4 5.2 %collective-permute-start.29 = (f32[128,128]{1,0:T(8,128)S(1)}, f32[128,128]{1,0:T(8,128)S(1)}, u32[]{:S(2)}, u32[]{:S(2)}) collective-permute-start(f32[128,128]{1,0:T(8,128)S(1)} %add.61), channel_id=1, source_target_pairs={{0,2},{1,3},{2,0},{3,1},{4,6},{5,7},{6,4},{7,5},{8,10},{9,11},{10,... | collective-permute-start | bytes 196616 | tf_op jit(solution)/shard_map/ppermute | solution.py:205
  129.7 5.4 %collective-permute-start.30 = (f32[128,128]{1,0:T(8,128)S(1)}, f32[128,128]{1,0:T(8,128)S(1)}, u32[]{:S(2)}, u32[]{:S(2)}) collective-permute-start(f32[128,128]{1,0:T(8,128)S(1)} %add.62), channel_id=1, source_target_pairs={{0,4},{1,5},{2,6},{3,7},{4,0},{5,1},{6,2},{7,3},{8,12},{9,13},{10,... | collective-permute-start | bytes 196616 | tf_op jit(solution)/shard_map/ppermute | solution.py:205
  135.1 5.4 %collective-permute-start.31 = (f32[128,128]{1,0:T(8,128)S(1)}, f32[128,128]{1,0:T(8,128)S(1)}, u32[]{:S(2)}, u32[]{:S(2)}) collective-permute-start(f32[128,128]{1,0:T(8,128)S(1)} %add.63), channel_id=1, source_target_pairs={{0,8},{1,9},{2,10},{3,11},{4,12},{5,13},{6,14},{7,15},{8,0},{9,1},... | collective-permute-start | bytes 196616 | tf_op jit(solution)/shard_map/ppermute | solution.py:205
  147.4 5.8 %collective-permute-start.34 = (bf16[4,64,32]{2,1,0:T(8,128)(2,1)S(1)}, bf16[4,64,32]{2,1,0:T(8,128)(2,1)S(1)}, u32[]{:S(2)}, u32[]{:S(2)}) collective-permute-start(bf16[4,64,32]{2,1,0:T(8,128)(2,1)S(1)} %get-tuple-element.117), channel_id=1, source_target_pairs={{0,1},{1,0},{2,3},{3,2},{4,5},{5,4},{6,7},{7,6},{8,9},{9,8},{10,11... | collective-permute-start | bytes 49160 | tf_op jit(solution)/shard_map/ppermute | solution.py:199
  154.5 5.7 %collective-permute-start.36 = (bf16[4,64,32]{2,1,0:T(8,128)(2,1)S(1)}, bf16[4,64,32]{2,1,0:T(8,128)(2,1)S(1)}, u32[]{:S(2)}, u32[]{:S(2)}) collective-permute-start(bf16[4,64,32]{2,1,0:T(8,128)(2,1)S(1)} %get-tuple-element.120), channel_id=1, source_target_pairs={{0,1},{1,0},{2,3},{3,2},{4,5},{5,4},{6,7},{7,6},{8,9},{9,8},{10,11... | collective-permute-start | bytes 49160 | tf_op jit(solution)/shard_map/ppermute | solution.py:199
  161.8 6.6 %collective-permute-start.38 = (f32[128,128]{1,0:T(8,128)S(1)}, f32[128,128]{1,0:T(8,128)S(1)}, u32[]{:S(2)}, u32[]{:S(2)}) collective-permute-start(f32[128,128]{1,0:T(8,128)S(1)} %get-tuple-element.125), channel_id=1, source_target_pairs={{0,1},{1,0},{2,3},{3,2},{4,5},{5,4},{6,7},{7,6},{8,9},{9,8},{10,11... | collective-permute-start | bytes 196616 | tf_op jit(solution)/shard_map/ppermute | solution.py:205
  168.4 5.3 %collective-permute-start.39 = (f32[128,128]{1,0:T(8,128)S(1)}, f32[128,128]{1,0:T(8,128)S(1)}, u32[]{:S(2)}, u32[]{:S(2)}) collective-permute-start(f32[128,128]{1,0:T(8,128)S(1)} %add.65), channel_id=1, source_target_pairs={{0,2},{1,3},{2,0},{3,1},{4,6},{5,7},{6,4},{7,5},{8,10},{9,11},{10,... | collective-permute-start | bytes 196616 | tf_op jit(solution)/shard_map/ppermute | solution.py:205
  173.7 5.5 %collective-permute-start.40 = (f32[128,128]{1,0:T(8,128)S(1)}, f32[128,128]{1,0:T(8,128)S(1)}, u32[]{:S(2)}, u32[]{:S(2)}) collective-permute-start(f32[128,128]{1,0:T(8,128)S(1)} %add.66), channel_id=1, source_target_pairs={{0,4},{1,5},{2,6},{3,7},{4,0},{5,1},{6,2},{7,3},{8,12},{9,13},{10,... | collective-permute-start | bytes 196616 | tf_op jit(solution)/shard_map/ppermute | solution.py:205
  179.2 5.4 %collective-permute-start.41 = (f32[128,128]{1,0:T(8,128)S(1)}, f32[128,128]{1,0:T(8,128)S(1)}, u32[]{:S(2)}, u32[]{:S(2)}) collective-permute-start(f32[128,128]{1,0:T(8,128)S(1)} %add.67), channel_id=1, source_target_pairs={{0,8},{1,9},{2,10},{3,11},{4,12},{5,13},{6,14},{7,15},{8,0},{9,1},... | collective-permute-start | bytes 196616 | tf_op jit(solution)/shard_map/ppermute | solution.py:205
  (22 other events, 30.7 us)

commit v3 on v2

v3 whole, which is shorter than its diff:
```python
import jax
import jax.numpy as jnp
from jax import lax
from jax.experimental import pallas as pl
from jax.experimental.pallas import tpu as pltpu
from jax.sharding import PartitionSpec as P

DOF = 64
FACES = 6
RHS = 32
SSTEP = 3
CYCLES = 4
MERGED = 2
POWERS = SSTEP * MERGED
GROWTH = 8.0
PACK = 4
META = 16
AXES = ("leaf", "sub")
F32 = jnp.float32
BF16 = jnp.bfloat16

VMEM = pl.BlockSpec(memory_space=pltpu.VMEM)
SMEM = pl.BlockSpec(memory_space=pltpu.SMEM)
PARAMS = pltpu.CompilerParams(vmem_limit_bytes=16 * 1024 * 1024)


def pack(message, blocks):
    for g in range(len(blocks) // PACK):
        message[g] = jnp.concatenate(blocks[PACK * g : PACK * g + PACK], axis=1).astype(BF16)


def unpack(ext, start, message):
    for g in range(message.shape[0]):
        row = message[g]
        for j in range(PACK):
            ext[start + PACK * g + j] = row[:, RHS * j : RHS * j + RHS]


def coupled(table, e, rows, ext):
    gathered = jnp.concatenate([ext[table[e, f]] for f in range(FACES)], axis=0)
    return jnp.dot(rows, gathered, preferred_element_type=F32)


def split(value):
    high = value.astype(BF16)
    return high, (value - high.astype(F32)).astype(BF16)


def listed(lists, side, ext):
    return [ext[lists[side, s]].astype(F32) for s in range(lists.shape[1])]


def start_kernel(lists, x, to_chip, to_link, ext):
    count = x.shape[0]
    ext[:count] = x[...].astype(BF16)
    ext[count] = jnp.zeros(ext.shape[1:], BF16)
    pack(to_chip, listed(lists, 0, ext))
    pack(to_link, listed(lists, 1, ext))


def rows_kernel(lists, positions, couple, to_chip, to_link):
    count = couple.shape[0]
    lanes = lax.broadcasted_iota(jnp.int32, (META, couple.shape[2]), 1)
    for side, message in ((0, to_chip), (1, to_link)):
        for s in range(message.shape[0]):
            place = lists[side, s]
            live = place < count
            e = jnp.minimum(place, count - 1)
            message[s, :DOF] = couple[e]
            nowhere = count + 2 * message.shape[0]
            values = [jnp.where(live, positions[e, f], nowhere) for f in range(FACES)] + [place]
            meta = jnp.zeros(lanes.shape, jnp.int32)
            for f, value in enumerate(values):
                meta = jnp.where(lanes == f, value, meta)
            message[s, DOF:] = meta.astype(F32).astype(BF16)


def residual_kernel(lists, positions, couple, from_chip, from_link, b, x, r, own, to_chip, ext):
    count = x.shape[0]
    ext[:count] = x[...].astype(BF16)
    unpack(ext, count, from_chip)
    unpack(ext, count + PACK * from_chip.shape[0], from_link)
    ext[ext.shape[0] - 1] = jnp.zeros(ext.shape[1:], BF16)
    for e in range(count):
        r[e] = b[e] - x[e] + coupled(positions, e, couple[e], ext)
    pack(own, [r[e] for e in range(count)])
    ext[:count] = r[...].astype(BF16)
    ext[count] = jnp.zeros(ext.shape[1:], BF16)
    pack(to_chip, listed(lists, 0, ext))


def extend(ext, mine, theirs):
    unpack(ext, 0, mine)
    unpack(ext, PACK * mine.shape[0], theirs)
    ext[ext.shape[0] - 1] = jnp.zeros(ext.shape[1:], BF16)


def power_kernel(table, couple, extra, mine, theirs, power, message, ext):
    count, slots = couple.shape[0], extra.shape[0]
    extend(ext, mine, theirs)
    values = []
    for e in range(count + slots):
        rows = couple[e] if e < count else extra[e - count, :DOF]
        values.append(coupled(table, e, rows, ext) * (1.0 / GROWTH))
        if e < count:
            power[e] = values[e]
    pack(message, values)


def gram_kernel(table, couple, mine, theirs, *refs):
    fields, (last, packed, ext) = refs[:POWERS], refs[POWERS:]
    count = couple.shape[0]
    rows = count * DOF
    extend(ext, mine, theirs)
    for e in range(count):
        last[e] = coupled(table, e, couple[e], ext) * (1.0 / GROWTH)
    fields = [field[...].reshape(rows, RHS) for field in (*fields, last)]
    images = [fields[k] - GROWTH * fields[k + 1] for k in range(POWERS)]
    stacked = jnp.concatenate(images + [fields[0], jnp.zeros((rows, RHS), F32)], axis=1)
    high, low = split(stacked)
    width = stacked.shape[1]
    sums = lax.dot_general(
        high, jnp.concatenate([high, low], axis=1), (((0,), (0,)), ((), ())), preferred_element_type=F32
    )
    cross = sums[:, width:]
    gram = sums[:, :width] + cross + cross.T
    half = width // 2
    below = jnp.concatenate([jnp.zeros((RHS, half), F32), gram[half : width - RHS, half:]], axis=0)
    packed[:, :half] = jnp.where(block_of(half, 0) > block_of(half, 1), below, gram[:half, :half])
    packed[:, half:] = gram[:half, half:]


def block_of(size, dimension):
    return lax.broadcasted_iota(jnp.int32, (size, size), dimension) // RHS


def unpack_gram(packed):
    half = packed.shape[0]
    low_left, right = packed[:, :half], packed[:, half:]
    row, column = block_of(half, 0), block_of(half, 1)
    first = jnp.where(row <= column, low_left, low_left.T)
    moved = jnp.concatenate([low_left[RHS:], jnp.zeros((RHS, half), F32)], axis=0)
    last = jnp.where(row >= column, moved, moved.T)
    last = jnp.where((row < 3) & (column < 3), last, 0.0)
    return jnp.concatenate(
        [jnp.concatenate([first, right], axis=1), jnp.concatenate([right.T, last], axis=1)], axis=0
    )


def eliminate(gram):
    count = SSTEP * RHS // 8
    groups = [gram[8 * g : 8 * g + 8, :] for g in range(count)]
    shape = groups[0].shape
    row_ids = lax.broadcasted_iota(jnp.int32, shape, 0)
    for home in range(count):
        columns = [
            [jnp.broadcast_to(group[:, 8 * home + m : 8 * home + m + 1], shape) for m in range(8)]
            for group in groups
        ]
        own = list(columns[home])
        panel = groups[home]
        for m in range(8):
            inverse = 1.0 / own[m][m : m + 1, :]
            scaled = panel[m : m + 1, :] * inverse
            panel = jnp.where(row_ids == m, scaled, panel - own[m] * scaled)
            for k in range(m + 1, 8):
                scaled = own[k][m : m + 1, :] * inverse
                own[k] = jnp.where(row_ids == m, scaled, own[k] - own[m] * scaled)
        for g in range(count):
            if g == home:
                groups[g] = panel
                continue
            for m in range(8):
                groups[g] = groups[g] - columns[g][m] * panel[m : m + 1, :]
    return jnp.concatenate(groups, axis=0)[:, SSTEP * RHS :]


def exact(a, b, contract=(1, 0)):
    return lax.dot_general(
        a,
        b,
        (((contract[0],), (contract[1],)), ((), ())),
        precision=lax.Precision.HIGHEST,
        preferred_element_type=F32,
    )


def below(value, size, blocks):
    parts = [jnp.zeros((RHS * blocks, value.shape[1]), F32)] if blocks else []
    rest = size - RHS * blocks - value.shape[0]
    parts.append(value)
    if rest:
        parts.append(jnp.zeros((rest, value.shape[1]), F32))
    return jnp.concatenate(parts, axis=0)


def mixing(packed):
    gram = unpack_gram(packed)
    size = gram.shape[0]
    right = RHS * POWERS
    square = SSTEP * RHS
    eye = (
        lax.broadcasted_iota(jnp.int32, (RHS, RHS), 0) == lax.broadcasted_iota(jnp.int32, (RHS, RHS), 1)
    ).astype(F32)

    first = eliminate(jnp.concatenate([gram[:square, :square], gram[:square, right : right + RHS]], axis=1))
    left = GROWTH * below(first, square + RHS, 1) - below(first, square + RHS, 0) + below(eye, square + RHS, 0)
    moved = jnp.concatenate([below(left, size, k) for k in range(SSTEP)], axis=1)
    images = jnp.concatenate([moved, below(eye, size, POWERS) - below(first, size, 0)], axis=1)
    second = eliminate(exact(images, exact(gram, images), (0, 0)))
    change = exact(moved, second)
    sol = below(first, size, 0) + change
    res = below(left, size, 0) - change + GROWTH * below(change[: size - RHS], size, 1)
    return jnp.concatenate([sol, res], axis=1)


def mixed(packed, fields):
    rows = fields[0].shape[0] * DOF
    mix_high, mix_low = split(mixing(packed))
    stacked = jnp.concatenate(
        [field[...].reshape(rows, RHS) for field in fields] + [jnp.zeros((rows, RHS), F32)], axis=1
    )
    high, low = split(stacked)
    out = jnp.dot(high, mix_high, preferred_element_type=F32)
    out += jnp.dot(high, mix_low, preferred_element_type=F32)
    out += jnp.dot(low, mix_high, preferred_element_type=F32)
    shape = fields[0].shape
    return out[:, :RHS].reshape(shape), out[:, RHS:].reshape(shape)


def update_kernel(lists, packed, *refs):
    fields, (x, new_x, r, own, to_chip, ext) = refs[: POWERS + 1], refs[POWERS + 1 :]
    count = x.shape[0]
    step, r[...] = mixed(packed, fields)
    new_x[...] = x[...] + step
    pack(own, [r[e] for e in range(count)])
    ext[:count] = r[...].astype(BF16)
    ext[count] = jnp.zeros(ext.shape[1:], BF16)
    pack(to_chip, listed(lists, 0, ext))


def finish_kernel(packed, *refs):
    fields, (x, new_x, r) = refs[: POWERS + 1], refs[POWERS + 1 :]
    step, r[...] = mixed(packed, fields)
    new_x[...] = x[...] + step


def shards(right_side, first_guess, couple, send_lists, neighbours):
    count = right_side.shape[0]
    slots = send_lists.shape[2]
    devices = lax.axis_size(AXES)
    assert lax.axis_size("sub") == 2 and slots % PACK == 0 and count % PACK == 0
    second = lax.axis_index("sub") == 1

    def shape(dtype, *sizes):
        return jax.ShapeDtypeStruct(sizes, dtype)

    field = shape(F32, count, DOF, RHS)
    slot_message = shape(BF16, slots // PACK, DOF, PACK * RHS)
    own_message = shape(BF16, count // PACK, DOF, PACK * RHS)
    message = shape(BF16, (count + slots) // PACK, DOF, PACK * RHS)
    row_message = shape(BF16, slots, DOF + META, FACES * DOF)
    gram_shape = shape(F32, (POWERS + 2) * RHS // 2, (POWERS + 2) * RHS)

    def call(kernel, outs, specs, name, blocks=0):
        return pl.pallas_call(
            kernel,
            out_shape=outs,
            in_specs=specs,
            out_specs=[VMEM] * len(outs),
            scratch_shapes=[pltpu.VMEM((blocks, DOF, RHS), BF16)] if blocks else [],
            compiler_params=PARAMS,
            name=name,
        )

    chip_base, link_base, nowhere = count, count + slots, count + 2 * slots
    own_lists = jnp.where(send_lists[0] < 0, count, send_lists[0]).astype(jnp.int32)
    lists = jnp.where(second, own_lists[::-1], own_lists)
    swapped = jnp.where(neighbours < link_base, neighbours + slots, neighbours - slots)
    codes = jnp.where(second | (neighbours < count), neighbours, swapped)
    codes = jnp.where(neighbours < 0, nowhere, codes).astype(jnp.int32)

    chip_pairs = [(d, d ^ 1) for d in range(devices)]
    link_pairs = [(d, d + 1 if d % 2 else d - 1) for d in range(devices)]
    link_pairs = [(s, t) for s, t in link_pairs if 0 <= t < devices]

    def chip(value):
        return lax.ppermute(value, AXES, chip_pairs)

    def link(value):
        return lax.ppermute(value, AXES, link_pairs)

    def total(value):
        step = 1
        while step < devices:
            value = value + lax.ppermute(value, AXES, [(d, d ^ step) for d in range(devices)])
            step *= 2
        return value

    reach = count + slots
    empty = 2 * reach

    def looked_up(places, at, base):
        found = jnp.full(at.shape, empty, jnp.int32)
        for s in range(slots):
            found = jnp.where(at == base + s, places[s], found)
        return found

    def table(known_base, far_base, own_places, rows):
        their_codes = rows[:, DOF, :FACES].astype(jnp.int32)
        their_places = rows[:, DOF, FACES].astype(jnp.int32)

        def place(at, own, known, far):
            is_known = (at >= known_base) & (at < known_base + slots)
            return jnp.where(at < count, at + own, jnp.where(is_known, at - known_base + known, far))

        far = jnp.where(their_places < count, their_places + reach, empty)
        near = jnp.where(own_places < count, own_places, empty)
        mine = place(codes, 0, count, looked_up(far, codes, far_base))
        theirs = place(their_codes, reach, reach + count, looked_up(near, their_codes, far_base))
        return jnp.concatenate([mine, theirs], axis=0)

    start = call(start_kernel, [slot_message] * 2, [SMEM, VMEM], "start", count + 1)
    send_rows = call(rows_kernel, [row_message] * 2, [SMEM, SMEM, VMEM], "rows")
    first = call(
        residual_kernel,
        [field, own_message, slot_message],
        [SMEM, SMEM] + [VMEM] * 5,
        "first_residual",
        nowhere + 1,
    )
    power = call(power_kernel, [field, message], [SMEM] + [VMEM] * 4, "power", empty + 1)
    gram = call(gram_kernel, [field, gram_shape], [SMEM] + [VMEM] * (3 + POWERS), "power_and_gram", empty + 1)
    update = call(
        update_kernel,
        [field, field, own_message, slot_message],
        [SMEM] + [VMEM] * (POWERS + 3),
        "solve_update",
        count + 1,
    )
    finish = call(finish_kernel, [field, field], [VMEM] * (POWERS + 3), "solve_finish")

    b = right_side.reshape(count, DOF, RHS)
    x = first_guess.reshape(count, DOF, RHS)
    to_chip, to_link = start(lists, x)
    from_link = link(to_link)
    from_chip = chip(to_chip)
    chip_rows, link_rows = send_rows(lists, codes, couple)
    link_rows = link(link_rows)
    chip_rows = chip(chip_rows)
    r, own, to_chip = first(lists, codes, couple, from_chip, from_link, b, x)
    link_table = table(chip_base, link_base, lists[1], link_rows)
    chip_table = table(link_base, chip_base, lists[0], chip_rows)
    for group in range(CYCLES // MERGED):
        mine = jnp.concatenate([own, chip(to_chip)], axis=0)
        fields = [r]
        for k in range(POWERS - 1):
            if k % 2 == 0:
                value, mine = power(link_table, couple, link_rows, mine, link(mine))
            else:
                value, mine = power(chip_table, couple, chip_rows, mine, chip(mine))
            fields.append(value)
        value, partial = gram(chip_table, couple, mine, chip(mine), *fields)
        fields.append(value)
        sums = total(partial)
        if group + 1 < CYCLES // MERGED:
            x, r, own, to_chip = update(lists, sums, *fields, x)
        else:
            x, r = finish(sums, *fields, x)
    return x.reshape(right_side.shape), r.reshape(right_side.shape)


def solution(mesh):
    rows = ("grp", "leaf", "sub")
    placed = (P(rows, None), P(rows, None), P(rows, None, None), P(rows, None, None), P(rows, None))
    return jax.shard_map(
        shards,
        mesh=mesh,
        in_specs=placed,
        out_specs=(P(rows, None), P(rows, None)),
        check_vma=False,
    )
```

time: 190 us -> 154 us (0.81)
  starting transfers between devices: 114 us -> 60.6 us
  other arithmetic: 0.16 us -> 10.4 us
  Pallas kernels: 35.4 us -> 40.3 us
  local copies, waits for them, and re-layouts: 3.89 us -> 5.93 us
    ppermute x16 -> x8, starting transfers between devices: 57.2 us -> 14.4 us  [total(): lax.ppermute(value, AXES, [(d, d ^ step) for d in range(devices)])]
    ppermute x26 -> x18, starting transfers between devices: 56.7 us -> 46.2 us  [the longest x10 40.3 us: chip(): return lax.ppermute(value, AXES, chip_pairs)]
    select_n x1 -> x8, other arithmetic: 0.01 us -> 10.3 us  [the longest x3 7.57 us: place(): jnp.where(at < count, at + own, jnp.where(is_known, at - known_base + kno...]
    pallas_call x18 -> x17, Pallas kernels: 35.4 us -> 40.3 us  [the longest x6 9.68 us: shards(): value, mine = power(link_table, couple, link_rows, mine, link(mine))]
    ppermute x26 -> x18, waiting for transfers between devices: 3.52 us -> 6.63 us  [the longest x10 6.61 us: chip(): return lax.ppermute(value, AXES, chip_pairs)]
    ppermute x16 -> x8, waiting for transfers between devices: 32 us -> 28.9 us  [total(): lax.ppermute(value, AXES, [(d, d ^ step) for d in range(devices)])]
  transfers between devices with their start and end apart: 42 -> 26, of which waited for: 27 -> 15; matrix products, arithmetic and copies ran while one was open for 0% -> 8% of each run, Pallas kernels for 0% -> 1%
where the time goes in v3:
time: 154 us
  starting transfers between devices  60.6 us (39%)
  Pallas kernels  40.3 us (26%)
  waiting for transfers between devices  35.6 us (23%)
  other arithmetic  10.4 us (7%)
  local copies, waits for them, and re-layouts  5.93 us (4%)
    ppermute x10, starting transfers between devices, chip(): return lax.ppermute(value, AXES, chip_pairs)  40.3 us
    ppermute x8, waiting for transfers between devices, total(): lax.ppermute(value, AXES, [(d, d ^ step) for d in range(devices)])  28.9 us
    ppermute x8, starting transfers between devices, total(): lax.ppermute(value, AXES, [(d, d ^ step) for d in range(devices)])  14.4 us
    pallas_call x6, Pallas kernels, shards(): value, mine = power(link_table, couple, link_rows, mine, link(mine))  9.68 us
    pallas_call x1, Pallas kernels, shards(): x, r, own, to_chip = update(lists, sums, *fields, x)  8.71 us
    pallas_call x1, Pallas kernels, shards(): x, r = finish(sums, *fields, x)  7.82 us
    select_n x3, other arithmetic, place(): jnp.where(at < count, at + own, jnp.where(is_known, at - known_base + kno...  7.57 us
    ppermute x10, waiting for transfers between devices, chip(): return lax.ppermute(value, AXES, chip_pairs)  6.61 us
  transfers between devices with their start and end apart: 26, of which 15 were waited for; matrix products, arithmetic and copies ran while one was open for 8% of the time, Pallas kernels for 1%

profile of v3, /device:TPU:0, one launch (start us, length us, event | category | flops | bytes accessed | tf_op | source)
XLA Modules:
  0.0 153.9 jit_solution(4298521570190880838)
XLA Ops:
  5.5 4.0 %collective-permute-start.2 = (bf16[1,64,128]{2,1,0:T(8,128)(2,1)S(1)}, bf16[1,64,128]{2,1,0:T(8,128)(2,1)S(1)}, u32[]{:S(2)}, u32[]{:S(2)}) collective-permute-start(bf16[1,64,128]{2,1,0:T(8,128)(2,1)S(1)} %get-tuple-element.41), channel_id=1, source_target_pairs={{0,1},{1,0},{2,3},{3,2},{4,5},{5,4},{6,7},{7,6},{8,9},{9,8},{10,11... | collective-permute-start | bytes 49160 | tf_op jit(solution)/shard_map/ppermute | solution.py:288
  12.5 3.6 %collective-permute-start.4 = (bf16[1,64,128]{2,1,0:T(8,128)(2,1)S(1)}, bf16[1,64,128]{2,1,0:T(8,128)(2,1)S(1)}, u32[]{:S(2)}, u32[]{:S(2)}) collective-permute-start(bf16[1,64,128]{2,1,0:T(8,128)(2,1)S(1)} %get-tuple-element.44), channel_id=1, source_target_pairs={{0,1},{1,0},{2,3},{3,2},{4,5},{5,4},{6,7},{7,6},{8,9},{9,8},{10,11... | collective-permute-start | bytes 49160 | tf_op jit(solution)/shard_map/ppermute | solution.py:288
  19.0 2.5 %compare_select_fusion.5 = (s32[4,1,6]{2,1,0:T(1,128)S(1)}, s32[4,1,6]{2,1,0:T(1,128)S(1)}) fusion(s32[]{:T(128)} %bitcast.17, s32[]{:T(128)} %bitcast.18, s32[]{:T(128)} %bitcast.20, s32[]{:T(128)} %bitcast.19, bf16[4,80,384]{2,1,0:T(8,128)(2,1)S(1)} %collective-permute-done.1.extra), kind=kLoop, calls=%fused_computation.12 | loop fusion | flops 240 | bytes 256 | tf_op jit(solution)/shard_map/jit(_where)/select_n | solution.py:306
  21.5 5.0 %compare_select_fusion = (s32[16,6]{1,0:T(8,128)S(1)}, s32[16,6]{1,0:T(8,128)S(1)}) fusion(s32[]{:T(128)} %bitcast.14, s32[]{:T(128)} %bitcast.13, s32[]{:T(128)} %bitcast.12, s32[]{:T(128)} %bitcast.11, s32[]{:T(128)} %bitcast.4, s32[]{:T(128)} %bitcast.3, s32[]{:T(128)} %bitcast.2, s32[]{:T(128)} %bitcast.1, s32[16,6]{1,0:T(8,128)S(1)} %copy.41, pred[]{:T(512)S(6)} %eq.85), kind=kLoop, calls=%fused_computation | loop fusion | flops 3552 | bytes 1185 | tf_op jit(solution)/shard_map/jit(_where)/select_n | solution.py:315
  28.2 4.0 %collective-permute-start.6 = (bf16[5,64,128]{2,1,0:T(8,128)(2,1)S(1)}, bf16[5,64,128]{2,1,0:T(8,128)(2,1)S(1)}, u32[]{:S(2)}, u32[]{:S(2)}) collective-permute-start(bf16[5,64,128]{2,1,0:T(8,128)(2,1)S(1)} %get-tuple-element.45.mine), channel_id=1, source_target_pairs={{0,1},{1,0},{2,3},{3,2},{4,5},{5,4},{6,7},{7,6},{8,9},{9,8},{10,11... | collective-permute-start | bytes 245768 | tf_op jit(solution)/shard_map/ppermute | solution.py:288
  32.2 2.5 %compare_select_fusion.11 = s32[4,1,6]{2,1,0:T(1,128)S(1)} fusion(bf16[4,80,384]{2,1,0:T(8,128)(2,1)S(1)} %collective-permute-done.extra, s32[]{:T(128)} %bitcast.6, s32[]{:T(128)} %bitcast.7, s32[]{:T(128)} %bitcast.9, s32[]{:T(128)} %bitcast.8), kind=kLoop, calls=%fused_computation.20 | loop fusion | flops 408 | bytes 160 | tf_op jit(solution)/shard_map/jit(_where)/select_n | solution.py:315
  38.7 5.4 %collective-permute-start.8 = (bf16[5,64,128]{2,1,0:T(8,128)(2,1)S(1)}, bf16[5,64,128]{2,1,0:T(8,128)(2,1)S(1)}, u32[]{:S(2)}, u32[]{:S(2)}) collective-permute-start(bf16[5,64,128]{2,1,0:T(8,128)(2,1)S(1)} %get-tuple-element.47.mine), channel_id=1, source_target_pairs={{0,1},{1,0},{2,3},{3,2},{4,5},{5,4},{6,7},{7,6},{8,9},{9,8},{10,11... | collective-permute-start | bytes 245768 | tf_op jit(solution)/shard_map/ppermute | solution.py:288
  49.1 5.9 %collective-permute-start.10 = (bf16[5,64,128]{2,1,0:T(8,128)(2,1)S(1)}, bf16[5,64,128]{2,1,0:T(8,128)(2,1)S(1)}, u32[]{:S(2)}, u32[]{:S(2)}) collective-permute-start(bf16[5,64,128]{2,1,0:T(8,128)(2,1)S(1)} %get-tuple-element.49.mine), channel_id=1, source_target_pairs={{0,1},{1,0},{2,3},{3,2},{4,5},{5,4},{6,7},{7,6},{8,9},{9,8},{10,11... | collective-permute-start | bytes 245768 | tf_op jit(solution)/shard_map/ppermute | solution.py:288
  55.9 2.4 %power_and_gram.2 = (f32[16,64,32]{2,1,0:T(8,128)S(1)}, f32[128,256]{1,0:T(8,128)S(1)}) custom-call(s32[20,6]{1,0:T(8,128)S(1)} %pad_add_fusion.table, bf16[16,64,384]{2,1,0:T(8,128)(2,1)S(1)} %copy-done.1, bf16[5,64,128]{2,1,0:T(8,128)(2,1)S(1)} %get-tuple-element.49.mine, bf16[5,64,128]{2,1,0:T(8,128)(2,1)S(1)} %collective-permute-done.10.theirs, ...), custom_call_target="tpu_custom_call" | custom-call | tf_op jit(solution)/shard_map/power_and_gram/pallas_call | solution.py:363
  59.8 2.9 %collective-permute-start.12 = (f32[128,256]{1,0:T(8,128)S(1)}, f32[128,256]{1,0:T(8,128)S(1)}, u32[]{:S(2)}, u32[]{:S(2)}) collective-permute-start(f32[128,256]{1,0:T(8,128)S(1)} %add.81), channel_id=1, source_target_pairs={{0,2},{1,3},{2,0},{3,1},{4,6},{5,7},{6,4},{7,5},{8,10},{9,11},{10,... | collective-permute-start | bytes 393224 | tf_op jit(solution)/shard_map/ppermute | solution.py:296
  62.7 4.0 %collective-permute-done.12 = f32[128,256]{1,0:T(8,128)S(1)} collective-permute-done((f32[128,256]{1,0:T(8,128)S(1)}, f32[128,256]{1,0:T(8,128)S(1)}, u32[]{:S(2)}, u32[]{:S(2)}) %collective-permute-start.12) | collective-permute-done | bytes 131104 | tf_op jit(solution)/shard_map/ppermute | solution.py:296
  68.6 3.3 %collective-permute-done.13 = f32[128,256]{1,0:T(8,128)S(1)} collective-permute-done((f32[128,256]{1,0:T(8,128)S(1)}, f32[128,256]{1,0:T(8,128)S(1)}, u32[]{:S(2)}, u32[]{:S(2)}) %collective-permute-start.13) | collective-permute-done | bytes 131104 | tf_op jit(solution)/shard_map/ppermute | solution.py:296
  72.0 2.7 %collective-permute-start.14 = (f32[128,256]{1,0:T(8,128)S(1)}, f32[128,256]{1,0:T(8,128)S(1)}, u32[]{:S(2)}, u32[]{:S(2)}) collective-permute-start(f32[128,256]{1,0:T(8,128)S(1)} %add.83), channel_id=1, source_target_pairs={{0,8},{1,9},{2,10},{3,11},{4,12},{5,13},{6,14},{7,15},{8,0},{9,1},... | collective-permute-start | bytes 393224 | tf_op jit(solution)/shard_map/ppermute | solution.py:296
  74.7 5.4 %collective-permute-done.14 = f32[128,256]{1,0:T(8,128)S(1)} collective-permute-done((f32[128,256]{1,0:T(8,128)S(1)}, f32[128,256]{1,0:T(8,128)S(1)}, u32[]{:S(2)}, u32[]{:S(2)}) %collective-permute-start.14) | collective-permute-done | bytes 131104 | tf_op jit(solution)/shard_map/ppermute | solution.py:296
  80.1 8.7 %solve_update.1 = (f32[16,64,32]{2,1,0:T(8,128)S(1)}, f32[16,64,32]{2,1,0:T(8,128)S(1)}, bf16[4,64,128]{2,1,0:T(8,128)(2,1)S(1)}, bf16[1,64,128]{2,1,0:T(8,128)(2,1)S(1)}) custom-call(s32[2,4]{1,0:T(2,128)S(1)} %broadcast_select_fusion.lists, f32[128,256]{1,0:T(8,128)S(1)} %add.84.packed, f32[16,64,32]{2,1,0:T(8,128)S(1)} %get-tuple-element.50.refs_0_, ...), custom_call_target="tpu_custom_call" | custom-call | tf_op jit(solution)/shard_map/solve_update/pallas_call | solution.py:367
  92.3 5.3 %collective-permute-start.17 = (bf16[5,64,128]{2,1,0:T(8,128)(2,1)S(1)}, bf16[5,64,128]{2,1,0:T(8,128)(2,1)S(1)}, u32[]{:S(2)}, u32[]{:S(2)}) collective-permute-start(bf16[5,64,128]{2,1,0:T(8,128)(2,1)S(1)} %get-tuple-element.60.mine), channel_id=1, source_target_pairs={{0,1},{1,0},{2,3},{3,2},{4,5},{5,4},{6,7},{7,6},{8,9},{9,8},{10,11... | collective-permute-start | bytes 245768 | tf_op jit(solution)/shard_map/ppermute | solution.py:288
  102.7 5.3 %collective-permute-start.19 = (bf16[5,64,128]{2,1,0:T(8,128)(2,1)S(1)}, bf16[5,64,128]{2,1,0:T(8,128)(2,1)S(1)}, u32[]{:S(2)}, u32[]{:S(2)}) collective-permute-start(bf16[5,64,128]{2,1,0:T(8,128)(2,1)S(1)} %get-tuple-element.62.mine), channel_id=1, source_target_pairs={{0,1},{1,0},{2,3},{3,2},{4,5},{5,4},{6,7},{7,6},{8,9},{9,8},{10,11... | collective-permute-start | bytes 245768 | tf_op jit(solution)/shard_map/ppermute | solution.py:288
  112.8 6.4 %collective-permute-start.21 = (bf16[5,64,128]{2,1,0:T(8,128)(2,1)S(1)}, bf16[5,64,128]{2,1,0:T(8,128)(2,1)S(1)}, u32[]{:S(2)}, u32[]{:S(2)}) collective-permute-start(bf16[5,64,128]{2,1,0:T(8,128)(2,1)S(1)} %get-tuple-element.64.mine), channel_id=1, source_target_pairs={{0,1},{1,0},{2,3},{3,2},{4,5},{5,4},{6,7},{7,6},{8,9},{9,8},{10,11... | collective-permute-start | bytes 245768 | tf_op jit(solution)/shard_map/ppermute | solution.py:288
  120.1 2.4 %power_and_gram.3 = (f32[16,64,32]{2,1,0:T(8,128)S(1)}, f32[128,256]{1,0:T(8,128)S(1)}) custom-call(s32[20,6]{1,0:T(8,128)S(1)} %pad_add_fusion.table, bf16[16,64,384]{2,1,0:T(8,128)(2,1)S(1)} %copy-done.1, bf16[5,64,128]{2,1,0:T(8,128)(2,1)S(1)} %get-tuple-element.64.mine, bf16[5,64,128]{2,1,0:T(8,128)(2,1)S(1)} %collective-permute-done.21.theirs, ...), custom_call_target="tpu_custom_call" | custom-call | tf_op jit(solution)/shard_map/power_and_gram/pallas_call | solution.py:363
  123.9 2.9 %collective-permute-start.23 = (f32[128,256]{1,0:T(8,128)S(1)}, f32[128,256]{1,0:T(8,128)S(1)}, u32[]{:S(2)}, u32[]{:S(2)}) collective-permute-start(f32[128,256]{1,0:T(8,128)S(1)} %add.85), channel_id=1, source_target_pairs={{0,2},{1,3},{2,0},{3,1},{4,6},{5,7},{6,4},{7,5},{8,10},{9,11},{10,... | collective-permute-start | bytes 393224 | tf_op jit(solution)/shard_map/ppermute | solution.py:296
  126.9 4.0 %collective-permute-done.23 = f32[128,256]{1,0:T(8,128)S(1)} collective-permute-done((f32[128,256]{1,0:T(8,128)S(1)}, f32[128,256]{1,0:T(8,128)S(1)}, u32[]{:S(2)}, u32[]{:S(2)}) %collective-permute-start.23) | collective-permute-done | bytes 131104 | tf_op jit(solution)/shard_map/ppermute | solution.py:296
  131.8 4.3 %collective-permute-done.24 = f32[128,256]{1,0:T(8,128)S(1)} collective-permute-done((f32[128,256]{1,0:T(8,128)S(1)}, f32[128,256]{1,0:T(8,128)S(1)}, u32[]{:S(2)}, u32[]{:S(2)}) %collective-permute-start.24) | collective-permute-done | bytes 131104 | tf_op jit(solution)/shard_map/ppermute | solution.py:296
  138.3 5.9 %collective-permute-done.25 = f32[128,256]{1,0:T(8,128)S(1)} collective-permute-done((f32[128,256]{1,0:T(8,128)S(1)}, f32[128,256]{1,0:T(8,128)S(1)}, u32[]{:S(2)}, u32[]{:S(2)}) %collective-permute-start.25) | collective-permute-done | bytes 131104 | tf_op jit(solution)/shard_map/ppermute | solution.py:296
  144.3 7.8 %solve_finish.1 = (f32[16,64,32]{2,1,0:T(8,128)S(1)}, f32[16,64,32]{2,1,0:T(8,128)S(1)}) custom-call(f32[128,256]{1,0:T(8,128)S(1)} %add.88.packed, f32[16,64,32]{2,1,0:T(8,128)S(1)} %get-tuple-element.65.refs_0_, f32[16,64,32]{2,1,0:T(8,128)S(1)} %get-tuple-element.66.refs_1_, f32[16,64,32]{2,1,0:T(8,128)S(1)} %get-tuple-element.67.refs_2_, ...), custom_call_target="tpu_custom_call" | custom-call | tf_op jit(solution)/shard_map/solve_finish/pallas_call | solution.py:369
  (91 shorter events, 46.1 us)
Async XLA Ops:
  3.3 14.2 %collective-permute-start = (bf16[4,80,384]{2,1,0:T(8,128)(2,1)S(1)}, bf16[4,80,384]{2,1,0:T(8,128)(2,1)S(1)}, u32[]{:S(2)}, u32[]{:S(2)}) collective-permute-start(bf16[4,80,384]{2,1,0:T(8,128)(2,1)S(1)} %get-tuple-element.39), channel_id=1, source_target_pairs={{0,1},{1,0},{2,3},{3,2},{4,5},{5,4},{6,7},{7,6},{8,9},{9,8},{10,11... | collective-permute-start | bytes 737288 | tf_op jit(solution)/shard_map/ppermute | solution.py:288
  3.9 14.4 %collective-permute-start.1 = (bf16[4,80,384]{2,1,0:T(8,128)(2,1)S(1)}, bf16[4,80,384]{2,1,0:T(8,128)(2,1)S(1)}, u32[]{:S(2)}, u32[]{:S(2)}) collective-permute-start(bf16[4,80,384]{2,1,0:T(8,128)(2,1)S(1)} %get-tuple-element.40), channel_id=1, source_target_pairs={{1,2},{2,1},{3,4},{4,3},{5,6},{6,5},{7,8},{8,7},{9,10},{10,9},{11,... | collective-permute-start | bytes 737288 | tf_op jit(solution)/shard_map/ppermute | solution.py:291
  5.5 5.5 %collective-permute-start.2 = (bf16[1,64,128]{2,1,0:T(8,128)(2,1)S(1)}, bf16[1,64,128]{2,1,0:T(8,128)(2,1)S(1)}, u32[]{:S(2)}, u32[]{:S(2)}) collective-permute-start(bf16[1,64,128]{2,1,0:T(8,128)(2,1)S(1)} %get-tuple-element.41), channel_id=1, source_target_pairs={{0,1},{1,0},{2,3},{3,2},{4,5},{5,4},{6,7},{7,6},{8,9},{9,8},{10,11... | collective-permute-start | bytes 49160 | tf_op jit(solution)/shard_map/ppermute | solution.py:288
  9.5 1.5 collective-permute-start.3
  12.5 4.4 %collective-permute-start.4 = (bf16[1,64,128]{2,1,0:T(8,128)(2,1)S(1)}, bf16[1,64,128]{2,1,0:T(8,128)(2,1)S(1)}, u32[]{:S(2)}, u32[]{:S(2)}) collective-permute-start(bf16[1,64,128]{2,1,0:T(8,128)(2,1)S(1)} %get-tuple-element.44), channel_id=1, source_target_pairs={{0,1},{1,0},{2,3},{3,2},{4,5},{5,4},{6,7},{7,6},{8,9},{9,8},{10,11... | collective-permute-start | bytes 49160 | tf_op jit(solution)/shard_map/ppermute | solution.py:288
  16.9 9.6 %collective-permute-start.5 = (bf16[5,64,128]{2,1,0:T(8,128)(2,1)S(1)}, bf16[5,64,128]{2,1,0:T(8,128)(2,1)S(1)}, u32[]{:S(2)}, u32[]{:S(2)}) collective-permute-start(bf16[5,64,128]{2,1,0:T(8,128)(2,1)S(1)} %constant_dynamic-update-slice_fusion.mine), channel_id=1, source_target_pairs={{1,2},{2,1},{3,4},{4,3},{5,6},{6,5},{7,8},{8,7},{9,10},{10,9},{11,... | collective-permute-start | bytes 245768 | tf_op jit(solution)/shard_map/ppermute | solution.py:291
  28.2 6.6 %collective-permute-start.6 = (bf16[5,64,128]{2,1,0:T(8,128)(2,1)S(1)}, bf16[5,64,128]{2,1,0:T(8,128)(2,1)S(1)}, u32[]{:S(2)}, u32[]{:S(2)}) collective-permute-start(bf16[5,64,128]{2,1,0:T(8,128)(2,1)S(1)} %get-tuple-element.45.mine), channel_id=1, source_target_pairs={{0,1},{1,0},{2,3},{3,2},{4,5},{5,4},{6,7},{7,6},{8,9},{9,8},{10,11... | collective-permute-start | bytes 245768 | tf_op jit(solution)/shard_map/ppermute | solution.py:288
  38.7 6.3 %collective-permute-start.8 = (bf16[5,64,128]{2,1,0:T(8,128)(2,1)S(1)}, bf16[5,64,128]{2,1,0:T(8,128)(2,1)S(1)}, u32[]{:S(2)}, u32[]{:S(2)}) collective-permute-start(bf16[5,64,128]{2,1,0:T(8,128)(2,1)S(1)} %get-tuple-element.47.mine), channel_id=1, source_target_pairs={{0,1},{1,0},{2,3},{3,2},{4,5},{5,4},{6,7},{7,6},{8,9},{9,8},{10,11... | collective-permute-start | bytes 245768 | tf_op jit(solution)/shard_map/ppermute | solution.py:288
  46.6 0.9 collective-permute-start.9
  49.1 6.8 %collective-permute-start.10 = (bf16[5,64,128]{2,1,0:T(8,128)(2,1)S(1)}, bf16[5,64,128]{2,1,0:T(8,128)(2,1)S(1)}, u32[]{:S(2)}, u32[]{:S(2)}) collective-permute-start(bf16[5,64,128]{2,1,0:T(8,128)(2,1)S(1)} %get-tuple-element.49.mine), channel_id=1, source_target_pairs={{0,1},{1,0},{2,3},{3,2},{4,5},{5,4},{6,7},{7,6},{8,9},{9,8},{10,11... | collective-permute-start | bytes 245768 | tf_op jit(solution)/shard_map/ppermute | solution.py:288
  58.3 1.4 collective-permute-start.11
  59.8 7.0 %collective-permute-start.12 = (f32[128,256]{1,0:T(8,128)S(1)}, f32[128,256]{1,0:T(8,128)S(1)}, u32[]{:S(2)}, u32[]{:S(2)}) collective-permute-start(f32[128,256]{1,0:T(8,128)S(1)} %add.81), channel_id=1, source_target_pairs={{0,2},{1,3},{2,0},{3,1},{4,6},{5,7},{6,4},{7,5},{8,10},{9,11},{10,... | collective-permute-start | bytes 393224 | tf_op jit(solution)/shard_map/ppermute | solution.py:296
  66.7 5.2 %collective-permute-start.13 = (f32[128,256]{1,0:T(8,128)S(1)}, f32[128,256]{1,0:T(8,128)S(1)}, u32[]{:S(2)}, u32[]{:S(2)}) collective-permute-start(f32[128,256]{1,0:T(8,128)S(1)} %add.82), channel_id=1, source_target_pairs={{0,4},{1,5},{2,6},{3,7},{4,0},{5,1},{6,2},{7,3},{8,12},{9,13},{10,... | collective-permute-start | bytes 393224 | tf_op jit(solution)/shard_map/ppermute | solution.py:296
  72.0 8.1 %collective-permute-start.14 = (f32[128,256]{1,0:T(8,128)S(1)}, f32[128,256]{1,0:T(8,128)S(1)}, u32[]{:S(2)}, u32[]{:S(2)}) collective-permute-start(f32[128,256]{1,0:T(8,128)S(1)} %add.83), channel_id=1, source_target_pairs={{0,8},{1,9},{2,10},{3,11},{4,12},{5,13},{6,14},{7,15},{8,0},{9,1},... | collective-permute-start | bytes 393224 | tf_op jit(solution)/shard_map/ppermute | solution.py:296
  88.8 1.2 collective-permute-start.15
  92.3 6.2 %collective-permute-start.17 = (bf16[5,64,128]{2,1,0:T(8,128)(2,1)S(1)}, bf16[5,64,128]{2,1,0:T(8,128)(2,1)S(1)}, u32[]{:S(2)}, u32[]{:S(2)}) collective-permute-start(bf16[5,64,128]{2,1,0:T(8,128)(2,1)S(1)} %get-tuple-element.60.mine), channel_id=1, source_target_pairs={{0,1},{1,0},{2,3},{3,2},{4,5},{5,4},{6,7},{7,6},{8,9},{9,8},{10,11... | collective-permute-start | bytes 245768 | tf_op jit(solution)/shard_map/ppermute | solution.py:288
  100.2 0.9 collective-permute-start.18
  102.7 6.2 %collective-permute-start.19 = (bf16[5,64,128]{2,1,0:T(8,128)(2,1)S(1)}, bf16[5,64,128]{2,1,0:T(8,128)(2,1)S(1)}, u32[]{:S(2)}, u32[]{:S(2)}) collective-permute-start(bf16[5,64,128]{2,1,0:T(8,128)(2,1)S(1)} %get-tuple-element.62.mine), channel_id=1, source_target_pairs={{0,1},{1,0},{2,3},{3,2},{4,5},{5,4},{6,7},{7,6},{8,9},{9,8},{10,11... | collective-permute-start | bytes 245768 | tf_op jit(solution)/shard_map/ppermute | solution.py:288
  110.5 0.7 collective-permute-start.20
  112.8 7.3 %collective-permute-start.21 = (bf16[5,64,128]{2,1,0:T(8,128)(2,1)S(1)}, bf16[5,64,128]{2,1,0:T(8,128)(2,1)S(1)}, u32[]{:S(2)}, u32[]{:S(2)}) collective-permute-start(bf16[5,64,128]{2,1,0:T(8,128)(2,1)S(1)} %get-tuple-element.64.mine), channel_id=1, source_target_pairs={{0,1},{1,0},{2,3},{3,2},{4,5},{5,4},{6,7},{7,6},{8,9},{9,8},{10,11... | collective-permute-start | bytes 245768 | tf_op jit(solution)/shard_map/ppermute | solution.py:288
  122.5 1.4 collective-permute-start.22
  123.9 7.0 %collective-permute-start.23 = (f32[128,256]{1,0:T(8,128)S(1)}, f32[128,256]{1,0:T(8,128)S(1)}, u32[]{:S(2)}, u32[]{:S(2)}) collective-permute-start(f32[128,256]{1,0:T(8,128)S(1)} %add.85), channel_id=1, source_target_pairs={{0,2},{1,3},{2,0},{3,1},{4,6},{5,7},{6,4},{7,5},{8,10},{9,11},{10,... | collective-permute-start | bytes 393224 | tf_op jit(solution)/shard_map/ppermute | solution.py:296
  130.9 5.2 %collective-permute-start.24 = (f32[128,256]{1,0:T(8,128)S(1)}, f32[128,256]{1,0:T(8,128)S(1)}, u32[]{:S(2)}, u32[]{:S(2)}) collective-permute-start(f32[128,256]{1,0:T(8,128)S(1)} %add.86), channel_id=1, source_target_pairs={{0,4},{1,5},{2,6},{3,7},{4,0},{5,1},{6,2},{7,3},{8,12},{9,13},{10,... | collective-permute-start | bytes 393224 | tf_op jit(solution)/shard_map/ppermute | solution.py:296
  136.2 8.1 %collective-permute-start.25 = (f32[128,256]{1,0:T(8,128)S(1)}, f32[128,256]{1,0:T(8,128)S(1)}, u32[]{:S(2)}, u32[]{:S(2)}) collective-permute-start(f32[128,256]{1,0:T(8,128)S(1)} %add.87), channel_id=1, source_target_pairs={{0,8},{1,9},{2,10},{3,11},{4,12},{5,13},{6,14},{7,15},{8,0},{9,1},... | collective-permute-start | bytes 393224 | tf_op jit(solution)/shard_map/ppermute | solution.py:296
  (8 other events, 19.1 us)

commit v4 on v3

--- a/solution.py
+++ b/solution.py
@@ -15,12 +15,13 @@
 GROWTH = 8.0
 PACK = 4
 META = 16
+LANES = 128
 AXES = ("leaf", "sub")
 F32 = jnp.float32
 BF16 = jnp.bfloat16
 
 VMEM = pl.BlockSpec(memory_space=pltpu.VMEM)
-SMEM = pl.BlockSpec(memory_space=pltpu.SMEM)
+ANY = pl.BlockSpec(memory_space=pl.ANY)
 PARAMS = pltpu.CompilerParams(vmem_limit_bytes=16 * 1024 * 1024)
 
 
@@ -47,7 +48,8 @@
 
 
 def listed(lists, side, ext):
-    return [ext[lists[side, s]].astype(F32) for s in range(lists.shape[1])]
+    slots = lists.shape[1] // 2
+    return [ext[lists[0, side * slots + s]].astype(F32) for s in range(slots)]
 
 
 def start_kernel(lists, x, to_chip, to_link, ext):
@@ -58,21 +60,40 @@
     pack(to_link, listed(lists, 1, ext))
 
 
-def rows_kernel(lists, positions, couple, to_chip, to_link):
-    count = couple.shape[0]
-    lanes = lax.broadcasted_iota(jnp.int32, (META, couple.shape[2]), 1)
+def rows_kernel(lists, codes, couple, after, to_chip, to_link):
+    count, slots = couple.shape[0], to_chip.shape[0]
+    lanes = lax.broadcasted_iota(jnp.int32, (1, LANES), 1)
     for side, message in ((0, to_chip), (1, to_link)):
-        for s in range(message.shape[0]):
-            place = lists[side, s]
-            live = place < count
+        for s in range(slots):
+            place = lists[0, side * slots + s]
             e = jnp.minimum(place, count - 1)
             message[s, :DOF] = couple[e]
-            nowhere = count + 2 * message.shape[0]
-            values = [jnp.where(live, positions[e, f], nowhere) for f in range(FACES)] + [place]
-            meta = jnp.zeros(lanes.shape, jnp.int32)
-            for f, value in enumerate(values):
-                meta = jnp.where(lanes == f, value, meta)
-            message[s, DOF:] = meta.astype(F32).astype(BF16)
+            meta = jnp.where(place < count, codes[pl.ds(e, 1), :], count + 2 * slots)
+            meta = jnp.where(lanes == FACES, place, meta).astype(F32)
+            message[s, DOF:] = jnp.zeros((META, couple.shape[2]), BF16)
+            message[s, DOF:, :LANES] = jnp.broadcast_to(meta, (META, LANES)).astype(BF16)
+
+
+def tables_kernel(lists, codes, chip_rows, link_rows, chip_table, link_table):
+    count, slots = codes.shape[0], chip_rows.shape[0]
+    reach = count + slots
+    chip_base, link_base, empty = count, count + slots, 2 * reach
+    sides = ((0, chip_table, chip_rows, link_base, chip_base), (1, link_table, link_rows, chip_base, link_base))
+    for side, table, rows, known_base, far_base in sides:
+        meta = [rows[s, DOF:, :LANES].astype(F32)[:1].astype(jnp.int32) for s in range(slots)]
+        far = [value[:, FACES : FACES + 1] for value in meta]
+        near = [lists[:, side * slots + s : side * slots + s + 1] for s in range(slots)]
+
+        def place(at, own, known, listed_at, listed_own):
+            found = jnp.where((at >= known_base) & (at < known_base + slots), at - known_base + known, empty)
+            for s in range(slots):
+                target = jnp.where(listed_at[s] < count, listed_at[s] + listed_own, empty)
+                found = jnp.where(at == far_base + s, target, found)
+            return jnp.where(at < count, at + own, found)
+
+        table[:count] = place(codes[...], 0, count, far, reach)
+        for s in range(slots):
+            table[count + s : count + s + 1] = place(meta[s], reach, reach + count, near, 0)
 
 
 def residual_kernel(lists, positions, couple, from_chip, from_link, b, x, r, own, to_chip, ext):
@@ -108,7 +129,7 @@
 
 
 def gram_kernel(table, couple, mine, theirs, *refs):
-    fields, (last, packed, ext) = refs[:POWERS], refs[POWERS:]
+    fields, (last, left, right, ext) = refs[:POWERS], refs[POWERS:]
     count = couple.shape[0]
     rows = count * DOF
     extend(ext, mine, theirs)
@@ -126,17 +147,17 @@
     gram = sums[:, :width] + cross + cross.T
     half = width // 2
     below = jnp.concatenate([jnp.zeros((RHS, half), F32), gram[half : width - RHS, half:]], axis=0)
-    packed[:, :half] = jnp.where(block_of(half, 0) > block_of(half, 1), below, gram[:half, :half])
-    packed[:, half:] = gram[:half, half:]
+    left[...] = jnp.where(block_of(half, 0) > block_of(half, 1), below, gram[:half, :half])
+    right[...] = gram[:half, half:]
 
 
 def block_of(size, dimension):
     return lax.broadcasted_iota(jnp.int32, (size, size), dimension) // RHS
 
 
-def unpack_gram(packed):
-    half = packed.shape[0]
-    low_left, right = packed[:, :half], packed[:, half:]
+def unpack_gram(left, right):
+    half = left.shape[0]
+    low_left, right = left[...], right[...]
     row, column = block_of(half, 0), block_of(half, 1)
     first = jnp.where(row <= column, low_left, low_left.T)
     moved = jnp.concatenate([low_left[RHS:], jnp.zeros((RHS, half), F32)], axis=0)
@@ -194,8 +215,8 @@
     return jnp.concatenate(parts, axis=0)
 
 
-def mixing(packed):
-    gram = unpack_gram(packed)
+def mixing(left, right):
+    gram = unpack_gram(left, right)
     size = gram.shape[0]
     right = RHS * POWERS
     square = SSTEP * RHS
@@ -204,19 +225,19 @@
     ).astype(F32)
 
     first = eliminate(jnp.concatenate([gram[:square, :square], gram[:square, right : right + RHS]], axis=1))
-    left = GROWTH * below(first, square + RHS, 1) - below(first, square + RHS, 0) + below(eye, square + RHS, 0)
-    moved = jnp.concatenate([below(left, size, k) for k in range(SSTEP)], axis=1)
+    first_left = GROWTH * below(first, square + RHS, 1) - below(first, square + RHS, 0) + below(eye, square + RHS, 0)
+    moved = jnp.concatenate([below(first_left, size, k) for k in range(SSTEP)], axis=1)
     images = jnp.concatenate([moved, below(eye, size, POWERS) - below(first, size, 0)], axis=1)
     second = eliminate(exact(images, exact(gram, images), (0, 0)))
     change = exact(moved, second)
     sol = below(first, size, 0) + change
-    res = below(left, size, 0) - change + GROWTH * below(change[: size - RHS], size, 1)
+    res = below(first_left, size, 0) - change + GROWTH * below(change[: size - RHS], size, 1)
     return jnp.concatenate([sol, res], axis=1)
 
 
-def mixed(packed, fields):
+def mixed(left, right, fields):
     rows = fields[0].shape[0] * DOF
-    mix_high, mix_low = split(mixing(packed))
+    mix_high, mix_low = split(mixing(left, right))
     stacked = jnp.concatenate(
         [field[...].reshape(rows, RHS) for field in fields] + [jnp.zeros((rows, RHS), F32)], axis=1
     )
@@ -228,10 +249,10 @@
     return out[:, :RHS].reshape(shape), out[:, RHS:].reshape(shape)
 
 
-def update_kernel(lists, packed, *refs):
+def update_kernel(lists, left, right, *refs):
     fields, (x, new_x, r, own, to_chip, ext) = refs[: POWERS + 1], refs[POWERS + 1 :]
     count = x.shape[0]
-    step, r[...] = mixed(packed, fields)
+    step, r[...] = mixed(left, right, fields)
     new_x[...] = x[...] + step
     pack(own, [r[e] for e in range(count)])
     ext[:count] = r[...].astype(BF16)
@@ -239,9 +260,9 @@
     pack(to_chip, listed(lists, 0, ext))
 
 
-def finish_kernel(packed, *refs):
+def finish_kernel(left, right, *refs):
     fields, (x, new_x, r) = refs[: POWERS + 1], refs[POWERS + 1 :]
-    step, r[...] = mixed(packed, fields)
+    step, r[...] = mixed(left, right, fields)
     new_x[...] = x[...] + step
 
 
@@ -260,7 +281,8 @@
     own_message = shape(BF16, count // PACK, DOF, PACK * RHS)
     message = shape(BF16, (count + slots) // PACK, DOF, PACK * RHS)
     row_message = shape(BF16, slots, DOF + META, FACES * DOF)
-    gram_shape = shape(F32, (POWERS + 2) * RHS // 2, (POWERS + 2) * RHS)
+    half_gram = shape(F32, (POWERS + 2) * RHS // 2, (POWERS + 2) * RHS // 2)
+    table_shape = shape(jnp.int32, count + slots, LANES)
 
     def call(kernel, outs, specs, name, blocks=0):
         return pl.pallas_call(
@@ -273,12 +295,13 @@
             name=name,
         )
 
-    chip_base, link_base, nowhere = count, count + slots, count + 2 * slots
+    nowhere = count + 2 * slots
     own_lists = jnp.where(send_lists[0] < 0, count, send_lists[0]).astype(jnp.int32)
-    lists = jnp.where(second, own_lists[::-1], own_lists)
-    swapped = jnp.where(neighbours < link_base, neighbours + slots, neighbours - slots)
+    lists = jnp.where(second, own_lists[::-1], own_lists).reshape(1, 2 * slots)
+    swapped = jnp.where(neighbours < count + slots, neighbours + slots, neighbours - slots)
     codes = jnp.where(second | (neighbours < count), neighbours, swapped)
     codes = jnp.where(neighbours < 0, nowhere, codes).astype(jnp.int32)
+    codes = jnp.pad(codes, ((0, 0), (0, LANES - FACES)))
 
     chip_pairs = [(d, d ^ 1) for d in range(devices)]
     link_pairs = [(d, d + 1 if d % 2 else d - 1) for d in range(devices)]
@@ -290,67 +313,49 @@
     def link(value):
         return lax.ppermute(value, AXES, link_pairs)
 
-    def total(value):
-        step = 1
+    def total(left, right):
+        value = jnp.where(second, right, left) + chip(jnp.where(second, left, right))
+        step = 2
         while step < devices:
             value = value + lax.ppermute(value, AXES, [(d, d ^ step) for d in range(devices)])
             step *= 2
-        return value
-
-    reach = count + slots
-    empty = 2 * reach
-
-    def looked_up(places, at, base):
-        found = jnp.full(at.shape, empty, jnp.int32)
-        for s in range(slots):
-            found = jnp.where(at == base + s, places[s], found)
-        return found
-
-    def table(known_base, far_base, own_places, rows):
-        their_codes = rows[:, DOF, :FACES].astype(jnp.int32)
-        their_places = rows[:, DOF, FACES].astype(jnp.int32)
-
-        def place(at, own, known, far):
-            is_known = (at >= known_base) & (at < known_base + slots)
-            return jnp.where(at < count, at + own, jnp.where(is_known, at - known_base + known, far))
-
-        far = jnp.where(their_places < count, their_places + reach, empty)
-        near = jnp.where(own_places < count, own_places, empty)
-        mine = place(codes, 0, count, looked_up(far, codes, far_base))
-        theirs = place(their_codes, reach, reach + count, looked_up(near, their_codes, far_base))
-        return jnp.concatenate([mine, theirs], axis=0)
-
-    start = call(start_kernel, [slot_message] * 2, [SMEM, VMEM], "start", count + 1)
-    send_rows = call(rows_kernel, [row_message] * 2, [SMEM, SMEM, VMEM], "rows")
+        other = chip(value)
+        return jnp.where(second, other, value), jnp.where(second, value, other)
+
+    start = call(start_kernel, [slot_message] * 2, [VMEM, VMEM], "start", count + 1)
+    send_rows = call(rows_kernel, [row_message] * 2, [VMEM, VMEM, VMEM, ANY], "rows")
+    tables = call(tables_kernel, [table_shape] * 2, [VMEM] * 4, "tables")
     first = call(
         residual_kernel,
         [field, own_message, slot_message],
-        [SMEM, SMEM] + [VMEM] * 5,
+        [VMEM] * 7,
         "first_residual",
         nowhere + 1,
     )
-    power = call(power_kernel, [field, message], [SMEM] + [VMEM] * 4, "power", empty + 1)
-    gram = call(gram_kernel, [field, gram_shape], [SMEM] + [VMEM] * (3 + POWERS), "power_and_gram", empty + 1)
+    reach = 2 * (count + slots) + 1
+    power = call(power_kernel, [field, message], [VMEM] * 5, "power", reach)
+    gram = call(
+        gram_kernel, [field, half_gram, half_gram], [VMEM] * (4 + POWERS), "power_and_gram", reach
+    )
     update = call(
         update_kernel,
         [field, field, own_message, slot_message],
-        [SMEM] + [VMEM] * (POWERS + 3),
+        [VMEM] * (POWERS + 5),
         "solve_update",
         count + 1,
     )
-    finish = call(finish_kernel, [field, field], [VMEM] * (POWERS + 3), "solve_finish")
+    finish = call(finish_kernel, [field, field], [VMEM] * (POWERS + 4), "solve_finish")
 
     b = right_side.reshape(count, DOF, RHS)
     x = first_guess.reshape(count, DOF, RHS)
     to_chip, to_link = start(lists, x)
     from_link = link(to_link)
     from_chip = chip(to_chip)
-    chip_rows, link_rows = send_rows(lists, codes, couple)
+    chip_rows, link_rows = send_rows(lists, codes, couple, from_chip)
     link_rows = link(link_rows)
     chip_rows = chip(chip_rows)
     r, own, to_chip = first(lists, codes, couple, from_chip, from_link, b, x)
-    link_table = table(chip_base, link_base, lists[1], link_rows)
-    chip_table = table(link_base, chip_base, lists[0], chip_rows)
+    chip_table, link_table = tables(lists, codes, chip_rows, link_rows)
     for group in range(CYCLES // MERGED):
         mine = jnp.concatenate([own, chip(to_chip)], axis=0)
         fields = [r]
@@ -360,13 +365,13 @@
             else:
                 value, mine = power(chip_table, couple, chip_rows, mine, chip(mine))
             fields.append(value)
-        value, partial = gram(chip_table, couple, mine, chip(mine), *fields)
+        value, left, right = gram(chip_table, couple, mine, chip(mine), *fields)
         fields.append(value)
-        sums = total(partial)
+        sums = total(left, right)
         if group + 1 < CYCLES // MERGED:
-            x, r, own, to_chip = update(lists, sums, *fields, x)
+            x, r, own, to_chip = update(lists, *sums, *fields, x)
         else:
-            x, r = finish(sums, *fields, x)
+            x, r = finish(*sums, *fields, x)
     return x.reshape(right_side.shape), r.reshape(right_side.shape)
 
 

time: 154 us -> 127 us (0.82)
  Pallas kernels: 40.3 us -> 30 us
  other arithmetic: 10.4 us -> 0.15 us
  waiting for transfers between devices: 35.6 us -> 25.9 us
  starting transfers between devices: 60.6 us -> 66.1 us
  local copies, waits for them, and re-layouts: 5.93 us -> 4.01 us
    ppermute x8 -> x6, waiting for transfers between devices: 28.9 us -> 14.2 us  [total(): lax.ppermute(value, AXES, [(d, d ^ step) for d in range(devices)])]
    select_n x8 -> x5, other arithmetic: 10.3 us -> 0.05 us  [the longest x2 0.02 us: total(): jnp.where(second, left, right)]
    ppermute x10 -> x14, waiting for transfers between devices: 6.61 us -> 11.7 us  [chip(): return lax.ppermute(value, AXES, chip_pairs)]
    pallas_call x6, Pallas kernels: 9.68 us -> 5.47 us  [shards(): value, mine = power(link_table, couple, link_rows, mine, link(mine))]
    ppermute x10 -> x14, starting transfers between devices: 40.3 us -> 43.6 us  [chip(): return lax.ppermute(value, AXES, chip_pairs)]
    pallas_call x4, Pallas kernels: 6.45 us -> 3.63 us  [shards(): value, mine = power(chip_table, couple, chip_rows, mine, chip(mine))]
    ppermute x8 -> x6, starting transfers between devices: 14.4 us -> 16.8 us  [total(): lax.ppermute(value, AXES, [(d, d ^ step) for d in range(devices)])]
    pallas_call x5 -> x6, Pallas kernels: 22.1 us -> 20 us  [the longest x1 8.2 us: shards(): x, r, own, to_chip = update(lists, *sums, *fields, x)]
  transfers between devices with their start and end apart: 26 -> 28, of which waited for: 15 -> 18; matrix products, arithmetic and copies ran while one was open for 8% -> 0% of each run, Pallas kernels for 1% -> 1%
where the time goes in v4:
time: 127 us
  starting transfers between devices  66.1 us (52%)
  Pallas kernels  30 us (24%)
  waiting for transfers between devices  25.9 us (20%)
  local copies, waits for them, and re-layouts  4.01 us (3%)
    ppermute x14, starting transfers between devices, chip(): return lax.ppermute(value, AXES, chip_pairs)  43.6 us
    ppermute x6, starting transfers between devices, total(): lax.ppermute(value, AXES, [(d, d ^ step) for d in range(devices)])  16.8 us
    ppermute x6, waiting for transfers between devices, total(): lax.ppermute(value, AXES, [(d, d ^ step) for d in range(devices)])  14.2 us
    ppermute x14, waiting for transfers between devices, chip(): return lax.ppermute(value, AXES, chip_pairs)  11.7 us
    pallas_call x1, Pallas kernels, shards(): x, r, own, to_chip = update(lists, *sums, *fields, x)  8.2 us
    pallas_call x1, Pallas kernels, shards(): x, r = finish(*sums, *fields, x)  7.83 us
    ppermute x8, starting transfers between devices, link(): return lax.ppermute(value, AXES, link_pairs)  5.68 us
    pallas_call x6, Pallas kernels, shards(): value, mine = power(link_table, couple, link_rows, mine, link(mine))  5.47 us
  transfers between devices with their start and end apart: 28, of which 18 were waited for; matrix products, arithmetic and copies ran while one was open for 0% of the time, Pallas kernels for 1%

profile of v4, /device:TPU:0, one launch (start us, length us, event | category | flops | bytes accessed | tf_op | source)
XLA Modules:
  0.0 127.1 jit_solution(11622225501535645133)
XLA Ops:
  4.5 4.0 %collective-permute-start.1 = (bf16[4,80,384]{2,1,0:T(8,128)(2,1)S(1)}, bf16[4,80,384]{2,1,0:T(8,128)(2,1)S(1)}, u32[]{:S(2)}, u32[]{:S(2)}) collective-permute-start(bf16[4,80,384]{2,1,0:T(8,128)(2,1)S(1)} %get-tuple-element.44), channel_id=1, source_target_pairs={{0,1},{1,0},{2,3},{3,2},{4,5},{5,4},{6,7},{7,6},{8,9},{9,8},{10,11... | collective-permute-start | bytes 737288 | tf_op jit(solution)/shard_map/ppermute | solution.py:311
  9.8 2.9 %collective-permute-start.4 = (bf16[1,64,128]{2,1,0:T(8,128)(2,1)S(1)}, bf16[1,64,128]{2,1,0:T(8,128)(2,1)S(1)}, u32[]{:S(2)}, u32[]{:S(2)}) collective-permute-start(bf16[1,64,128]{2,1,0:T(8,128)(2,1)S(1)} %get-tuple-element.50), channel_id=1, source_target_pairs={{0,1},{1,0},{2,3},{3,2},{4,5},{5,4},{6,7},{7,6},{8,9},{9,8},{10,11... | collective-permute-start | bytes 49160 | tf_op jit(solution)/shard_map/ppermute | solution.py:311
  15.3 5.3 %collective-permute-start.6 = (bf16[5,64,128]{2,1,0:T(8,128)(2,1)S(1)}, bf16[5,64,128]{2,1,0:T(8,128)(2,1)S(1)}, u32[]{:S(2)}, u32[]{:S(2)}) collective-permute-start(bf16[5,64,128]{2,1,0:T(8,128)(2,1)S(1)} %get-tuple-element.51.mine), channel_id=1, source_target_pairs={{0,1},{1,0},{2,3},{3,2},{4,5},{5,4},{6,7},{7,6},{8,9},{9,8},{10,11... | collective-permute-start | bytes 245768 | tf_op jit(solution)/shard_map/ppermute | solution.py:311
  24.1 5.9 %collective-permute-start.8 = (bf16[5,64,128]{2,1,0:T(8,128)(2,1)S(1)}, bf16[5,64,128]{2,1,0:T(8,128)(2,1)S(1)}, u32[]{:S(2)}, u32[]{:S(2)}) collective-permute-start(bf16[5,64,128]{2,1,0:T(8,128)(2,1)S(1)} %get-tuple-element.53.mine), channel_id=1, source_target_pairs={{0,1},{1,0},{2,3},{3,2},{4,5},{5,4},{6,7},{7,6},{8,9},{9,8},{10,11... | collective-permute-start | bytes 245768 | tf_op jit(solution)/shard_map/ppermute | solution.py:311
  33.6 6.2 %collective-permute-start.10 = (bf16[5,64,128]{2,1,0:T(8,128)(2,1)S(1)}, bf16[5,64,128]{2,1,0:T(8,128)(2,1)S(1)}, u32[]{:S(2)}, u32[]{:S(2)}) collective-permute-start(bf16[5,64,128]{2,1,0:T(8,128)(2,1)S(1)} %get-tuple-element.55.mine), channel_id=1, source_target_pairs={{0,1},{1,0},{2,3},{3,2},{4,5},{5,4},{6,7},{7,6},{8,9},{9,8},{10,11... | collective-permute-start | bytes 245768 | tf_op jit(solution)/shard_map/ppermute | solution.py:311
  40.8 1.8 %power_and_gram.2 = (f32[16,64,32]{2,1,0:T(8,128)S(1)}, f32[128,128]{1,0:T(8,128)S(1)}, f32[128,128]{1,0:T(8,128)S(1)}) custom-call(s32[20,128]{1,0:T(8,128)S(1)} %get-tuple-element.46.table, bf16[16,64,384]{2,1,0:T(8,128)(2,1)S(1)} %copy-done, bf16[5,64,128]{2,1,0:T(8,128)(2,1)S(1)} %get-tuple-element.55.mine, ...), custom_call_target="tpu_custom_call" | custom-call | tf_op jit(solution)/shard_map/power_and_gram/pallas_call | solution.py:368
  44.0 2.9 %collective-permute-start.12 = (f32[128,128]{1,0:T(8,128)S(1)}, f32[128,128]{1,0:T(8,128)S(1)}, u32[]{:S(2)}, u32[]{:S(2)}) collective-permute-start(f32[128,128]{1,0:T(8,128)S(1)} %select_add_fusion.1), channel_id=1, source_target_pairs={{0,2},{1,3},{2,0},{3,1},{4,6},{5,7},{6,4},{7,5},{8,10},{9,11},{10,... | collective-permute-start | bytes 196616 | tf_op jit(solution)/shard_map/ppermute | solution.py:320
  46.9 2.6 %collective-permute-done.12 = f32[128,128]{1,0:T(8,128)S(1)} collective-permute-done((f32[128,128]{1,0:T(8,128)S(1)}, f32[128,128]{1,0:T(8,128)S(1)}, u32[]{:S(2)}, u32[]{:S(2)}) %collective-permute-start.12) | collective-permute-done | bytes 65568 | tf_op jit(solution)/shard_map/ppermute | solution.py:320
  49.5 2.1 %collective-permute-start.13 = (f32[128,128]{1,0:T(8,128)S(1)}, f32[128,128]{1,0:T(8,128)S(1)}, u32[]{:S(2)}, u32[]{:S(2)}) collective-permute-start(f32[128,128]{1,0:T(8,128)S(1)} %add.32), channel_id=1, source_target_pairs={{0,4},{1,5},{2,6},{3,7},{4,0},{5,1},{6,2},{7,3},{8,12},{9,13},{10,... | collective-permute-start | bytes 196616 | tf_op jit(solution)/shard_map/ppermute | solution.py:320
  51.7 2.2 %collective-permute-done.13 = f32[128,128]{1,0:T(8,128)S(1)} collective-permute-done((f32[128,128]{1,0:T(8,128)S(1)}, f32[128,128]{1,0:T(8,128)S(1)}, u32[]{:S(2)}, u32[]{:S(2)}) %collective-permute-start.13) | collective-permute-done | bytes 65568 | tf_op jit(solution)/shard_map/ppermute | solution.py:320
  53.9 3.1 %collective-permute-start.14 = (f32[128,128]{1,0:T(8,128)S(1)}, f32[128,128]{1,0:T(8,128)S(1)}, u32[]{:S(2)}, u32[]{:S(2)}) collective-permute-start(f32[128,128]{1,0:T(8,128)S(1)} %add.33), channel_id=1, source_target_pairs={{0,8},{1,9},{2,10},{3,11},{4,12},{5,13},{6,14},{7,15},{8,0},{9,1},... | collective-permute-start | bytes 196616 | tf_op jit(solution)/shard_map/ppermute | solution.py:320
  57.0 2.2 %collective-permute-done.14 = f32[128,128]{1,0:T(8,128)S(1)} collective-permute-done((f32[128,128]{1,0:T(8,128)S(1)}, f32[128,128]{1,0:T(8,128)S(1)}, u32[]{:S(2)}, u32[]{:S(2)}) %collective-permute-start.14) | collective-permute-done | bytes 65568 | tf_op jit(solution)/shard_map/ppermute | solution.py:320
  60.6 8.2 %solve_update.1 = (f32[16,64,32]{2,1,0:T(8,128)S(1)}, f32[16,64,32]{2,1,0:T(8,128)S(1)}, bf16[4,64,128]{2,1,0:T(8,128)(2,1)S(1)}, bf16[1,64,128]{2,1,0:T(8,128)(2,1)S(1)}) custom-call(s32[1,8]{1,0:T(1,128)S(1)} %reshape.19.lists, f32[128,128]{1,0:T(8,128)S(1)} %get-tuple-element.87.left, f32[128,128]{1,0:T(8,128)S(1)} %get-tuple-element.86.right, ...), custom_call_target="tpu_custom_call" | custom-call | tf_op jit(solution)/shard_map/solve_update/pallas_call | solution.py:372
  71.6 5.3 %collective-permute-start.18 = (bf16[5,64,128]{2,1,0:T(8,128)(2,1)S(1)}, bf16[5,64,128]{2,1,0:T(8,128)(2,1)S(1)}, u32[]{:S(2)}, u32[]{:S(2)}) collective-permute-start(bf16[5,64,128]{2,1,0:T(8,128)(2,1)S(1)} %get-tuple-element.67.mine), channel_id=1, source_target_pairs={{0,1},{1,0},{2,3},{3,2},{4,5},{5,4},{6,7},{7,6},{8,9},{9,8},{10,11... | collective-permute-start | bytes 245768 | tf_op jit(solution)/shard_map/ppermute | solution.py:311
  80.6 5.8 %collective-permute-start.20 = (bf16[5,64,128]{2,1,0:T(8,128)(2,1)S(1)}, bf16[5,64,128]{2,1,0:T(8,128)(2,1)S(1)}, u32[]{:S(2)}, u32[]{:S(2)}) collective-permute-start(bf16[5,64,128]{2,1,0:T(8,128)(2,1)S(1)} %get-tuple-element.69.mine), channel_id=1, source_target_pairs={{0,1},{1,0},{2,3},{3,2},{4,5},{5,4},{6,7},{7,6},{8,9},{9,8},{10,11... | collective-permute-start | bytes 245768 | tf_op jit(solution)/shard_map/ppermute | solution.py:311
  89.8 6.4 %collective-permute-start.22 = (bf16[5,64,128]{2,1,0:T(8,128)(2,1)S(1)}, bf16[5,64,128]{2,1,0:T(8,128)(2,1)S(1)}, u32[]{:S(2)}, u32[]{:S(2)}) collective-permute-start(bf16[5,64,128]{2,1,0:T(8,128)(2,1)S(1)} %get-tuple-element.71.mine), channel_id=1, source_target_pairs={{0,1},{1,0},{2,3},{3,2},{4,5},{5,4},{6,7},{7,6},{8,9},{9,8},{10,11... | collective-permute-start | bytes 245768 | tf_op jit(solution)/shard_map/ppermute | solution.py:311
  97.1 1.8 %power_and_gram.3 = (f32[16,64,32]{2,1,0:T(8,128)S(1)}, f32[128,128]{1,0:T(8,128)S(1)}, f32[128,128]{1,0:T(8,128)S(1)}) custom-call(s32[20,128]{1,0:T(8,128)S(1)} %get-tuple-element.46.table, bf16[16,64,384]{2,1,0:T(8,128)(2,1)S(1)} %copy-done, bf16[5,64,128]{2,1,0:T(8,128)(2,1)S(1)} %get-tuple-element.71.mine, ...), custom_call_target="tpu_custom_call" | custom-call | tf_op jit(solution)/shard_map/power_and_gram/pallas_call | solution.py:368
  100.3 2.9 %collective-permute-start.24 = (f32[128,128]{1,0:T(8,128)S(1)}, f32[128,128]{1,0:T(8,128)S(1)}, u32[]{:S(2)}, u32[]{:S(2)}) collective-permute-start(f32[128,128]{1,0:T(8,128)S(1)} %select_add_fusion), channel_id=1, source_target_pairs={{0,2},{1,3},{2,0},{3,1},{4,6},{5,7},{6,4},{7,5},{8,10},{9,11},{10,... | collective-permute-start | bytes 196616 | tf_op jit(solution)/shard_map/ppermute | solution.py:320
  103.3 2.6 %collective-permute-done.24 = f32[128,128]{1,0:T(8,128)S(1)} collective-permute-done((f32[128,128]{1,0:T(8,128)S(1)}, f32[128,128]{1,0:T(8,128)S(1)}, u32[]{:S(2)}, u32[]{:S(2)}) %collective-permute-start.24) | collective-permute-done | bytes 65568 | tf_op jit(solution)/shard_map/ppermute | solution.py:320
  105.9 2.5 %collective-permute-start.25 = (f32[128,128]{1,0:T(8,128)S(1)}, f32[128,128]{1,0:T(8,128)S(1)}, u32[]{:S(2)}, u32[]{:S(2)}) collective-permute-start(f32[128,128]{1,0:T(8,128)S(1)} %add.36), channel_id=1, source_target_pairs={{0,4},{1,5},{2,6},{3,7},{4,0},{5,1},{6,2},{7,3},{8,12},{9,13},{10,... | collective-permute-start | bytes 196616 | tf_op jit(solution)/shard_map/ppermute | solution.py:320
  108.4 2.2 %collective-permute-done.25 = f32[128,128]{1,0:T(8,128)S(1)} collective-permute-done((f32[128,128]{1,0:T(8,128)S(1)}, f32[128,128]{1,0:T(8,128)S(1)}, u32[]{:S(2)}, u32[]{:S(2)}) %collective-permute-start.25) | collective-permute-done | bytes 65568 | tf_op jit(solution)/shard_map/ppermute | solution.py:320
  110.7 3.2 %collective-permute-start.26 = (f32[128,128]{1,0:T(8,128)S(1)}, f32[128,128]{1,0:T(8,128)S(1)}, u32[]{:S(2)}, u32[]{:S(2)}) collective-permute-start(f32[128,128]{1,0:T(8,128)S(1)} %add.37), channel_id=1, source_target_pairs={{0,8},{1,9},{2,10},{3,11},{4,12},{5,13},{6,14},{7,15},{8,0},{9,1},... | collective-permute-start | bytes 196616 | tf_op jit(solution)/shard_map/ppermute | solution.py:320
  113.9 2.2 %collective-permute-done.26 = f32[128,128]{1,0:T(8,128)S(1)} collective-permute-done((f32[128,128]{1,0:T(8,128)S(1)}, f32[128,128]{1,0:T(8,128)S(1)}, u32[]{:S(2)}, u32[]{:S(2)}) %collective-permute-start.26) | collective-permute-done | bytes 65568 | tf_op jit(solution)/shard_map/ppermute | solution.py:320
  117.5 7.8 %solve_finish.1 = (f32[16,64,32]{2,1,0:T(8,128)S(1)}, f32[16,64,32]{2,1,0:T(8,128)S(1)}) custom-call(f32[128,128]{1,0:T(8,128)S(1)} %get-tuple-element.85.left, f32[128,128]{1,0:T(8,128)S(1)} %get-tuple-element.84.right, f32[16,64,32]{2,1,0:T(8,128)S(1)} %get-tuple-element.72.refs_0_, f32[16,64,32]{2,1,0:T(8,128)S(1)} %get-tuple-element.73.refs_1_, ...), custom_call_target="tpu_custom_call" | custom-call | tf_op jit(solution)/shard_map/solve_finish/pallas_call | solution.py:374
  (85 shorter events, 33.5 us)
Async XLA Ops:
  2.8 1.5 %collective-permute-start = (bf16[1,64,128]{2,1,0:T(8,128)(2,1)S(1)}, bf16[1,64,128]{2,1,0:T(8,128)(2,1)S(1)}, u32[]{:S(2)}, u32[]{:S(2)}) collective-permute-start(bf16[1,64,128]{2,1,0:T(8,128)(2,1)S(1)} %get-tuple-element.43), channel_id=1, source_target_pairs={{0,1},{1,0},{2,3},{3,2},{4,5},{5,4},{6,7},{7,6},{8,9},{9,8},{10,11... | collective-permute-start | bytes 49160 | tf_op jit(solution)/shard_map/ppermute | solution.py:311
  3.3 5.8 %collective-permute-start.3 = (bf16[1,64,128]{2,1,0:T(8,128)(2,1)S(1)}, bf16[1,64,128]{2,1,0:T(8,128)(2,1)S(1)}, u32[]{:S(2)}, u32[]{:S(2)}) collective-permute-start(bf16[1,64,128]{2,1,0:T(8,128)(2,1)S(1)} %get-tuple-element.48), channel_id=1, source_target_pairs={{1,2},{2,1},{3,4},{4,3},{5,6},{6,5},{7,8},{8,7},{9,10},{10,9},{11,... | collective-permute-start | bytes 49160 | tf_op jit(solution)/shard_map/ppermute | solution.py:314
  4.5 9.8 %collective-permute-start.1 = (bf16[4,80,384]{2,1,0:T(8,128)(2,1)S(1)}, bf16[4,80,384]{2,1,0:T(8,128)(2,1)S(1)}, u32[]{:S(2)}, u32[]{:S(2)}) collective-permute-start(bf16[4,80,384]{2,1,0:T(8,128)(2,1)S(1)} %get-tuple-element.44), channel_id=1, source_target_pairs={{0,1},{1,0},{2,3},{3,2},{4,5},{5,4},{6,7},{7,6},{8,9},{9,8},{10,11... | collective-permute-start | bytes 737288 | tf_op jit(solution)/shard_map/ppermute | solution.py:311
  8.4 5.9 %collective-permute-start.2 = (bf16[4,80,384]{2,1,0:T(8,128)(2,1)S(1)}, bf16[4,80,384]{2,1,0:T(8,128)(2,1)S(1)}, u32[]{:S(2)}, u32[]{:S(2)}) collective-permute-start(bf16[4,80,384]{2,1,0:T(8,128)(2,1)S(1)} %get-tuple-element.45), channel_id=1, source_target_pairs={{1,2},{2,1},{3,4},{4,3},{5,6},{6,5},{7,8},{8,7},{9,10},{10,9},{11,... | collective-permute-start | bytes 737288 | tf_op jit(solution)/shard_map/ppermute | solution.py:314
  9.8 3.8 %collective-permute-start.4 = (bf16[1,64,128]{2,1,0:T(8,128)(2,1)S(1)}, bf16[1,64,128]{2,1,0:T(8,128)(2,1)S(1)}, u32[]{:S(2)}, u32[]{:S(2)}) collective-permute-start(bf16[1,64,128]{2,1,0:T(8,128)(2,1)S(1)} %get-tuple-element.50), channel_id=1, source_target_pairs={{0,1},{1,0},{2,3},{3,2},{4,5},{5,4},{6,7},{7,6},{8,9},{9,8},{10,11... | collective-permute-start | bytes 49160 | tf_op jit(solution)/shard_map/ppermute | solution.py:311
  15.3 6.3 %collective-permute-start.6 = (bf16[5,64,128]{2,1,0:T(8,128)(2,1)S(1)}, bf16[5,64,128]{2,1,0:T(8,128)(2,1)S(1)}, u32[]{:S(2)}, u32[]{:S(2)}) collective-permute-start(bf16[5,64,128]{2,1,0:T(8,128)(2,1)S(1)} %get-tuple-element.51.mine), channel_id=1, source_target_pairs={{0,1},{1,0},{2,3},{3,2},{4,5},{5,4},{6,7},{7,6},{8,9},{9,8},{10,11... | collective-permute-start | bytes 245768 | tf_op jit(solution)/shard_map/ppermute | solution.py:311
  24.1 6.9 %collective-permute-start.8 = (bf16[5,64,128]{2,1,0:T(8,128)(2,1)S(1)}, bf16[5,64,128]{2,1,0:T(8,128)(2,1)S(1)}, u32[]{:S(2)}, u32[]{:S(2)}) collective-permute-start(bf16[5,64,128]{2,1,0:T(8,128)(2,1)S(1)} %get-tuple-element.53.mine), channel_id=1, source_target_pairs={{0,1},{1,0},{2,3},{3,2},{4,5},{5,4},{6,7},{7,6},{8,9},{9,8},{10,11... | collective-permute-start | bytes 245768 | tf_op jit(solution)/shard_map/ppermute | solution.py:311
  31.9 0.9 collective-permute-start.9
  33.6 7.1 %collective-permute-start.10 = (bf16[5,64,128]{2,1,0:T(8,128)(2,1)S(1)}, bf16[5,64,128]{2,1,0:T(8,128)(2,1)S(1)}, u32[]{:S(2)}, u32[]{:S(2)}) collective-permute-start(bf16[5,64,128]{2,1,0:T(8,128)(2,1)S(1)} %get-tuple-element.55.mine), channel_id=1, source_target_pairs={{0,1},{1,0},{2,3},{3,2},{4,5},{5,4},{6,7},{7,6},{8,9},{9,8},{10,11... | collective-permute-start | bytes 245768 | tf_op jit(solution)/shard_map/ppermute | solution.py:311
  42.6 1.3 %collective-permute-start.11 = (f32[128,128]{1,0:T(8,128)S(1)}, f32[128,128]{1,0:T(8,128)S(1)}, u32[]{:S(2)}, u32[]{:S(2)}) collective-permute-start(f32[128,128]{1,0:T(8,128)S(1)} %broadcast_select_fusion.5), channel_id=1, source_target_pairs={{0,1},{1,0},{2,3},{3,2},{4,5},{5,4},{6,7},{7,6},{8,9},{9,8},{10,11... | collective-permute-start | bytes 196616 | tf_op jit(solution)/shard_map/ppermute | solution.py:311
  44.0 5.5 %collective-permute-start.12 = (f32[128,128]{1,0:T(8,128)S(1)}, f32[128,128]{1,0:T(8,128)S(1)}, u32[]{:S(2)}, u32[]{:S(2)}) collective-permute-start(f32[128,128]{1,0:T(8,128)S(1)} %select_add_fusion.1), channel_id=1, source_target_pairs={{0,2},{1,3},{2,0},{3,1},{4,6},{5,7},{6,4},{7,5},{8,10},{9,11},{10,... | collective-permute-start | bytes 196616 | tf_op jit(solution)/shard_map/ppermute | solution.py:320
  49.5 4.4 %collective-permute-start.13 = (f32[128,128]{1,0:T(8,128)S(1)}, f32[128,128]{1,0:T(8,128)S(1)}, u32[]{:S(2)}, u32[]{:S(2)}) collective-permute-start(f32[128,128]{1,0:T(8,128)S(1)} %add.32), channel_id=1, source_target_pairs={{0,4},{1,5},{2,6},{3,7},{4,0},{5,1},{6,2},{7,3},{8,12},{9,13},{10,... | collective-permute-start | bytes 196616 | tf_op jit(solution)/shard_map/ppermute | solution.py:320
  53.9 5.3 %collective-permute-start.14 = (f32[128,128]{1,0:T(8,128)S(1)}, f32[128,128]{1,0:T(8,128)S(1)}, u32[]{:S(2)}, u32[]{:S(2)}) collective-permute-start(f32[128,128]{1,0:T(8,128)S(1)} %add.33), channel_id=1, source_target_pairs={{0,8},{1,9},{2,10},{3,11},{4,12},{5,13},{6,14},{7,15},{8,0},{9,1},... | collective-permute-start | bytes 196616 | tf_op jit(solution)/shard_map/ppermute | solution.py:320
  59.3 1.3 %collective-permute-start.15 = (f32[128,128]{1,0:T(8,128)S(1)}, f32[128,128]{1,0:T(8,128)S(1)}, u32[]{:S(2)}, u32[]{:S(2)}) collective-permute-start(f32[128,128]{1,0:T(8,128)S(1)} %add.34), channel_id=1, source_target_pairs={{0,1},{1,0},{2,3},{3,2},{4,5},{5,4},{6,7},{7,6},{8,9},{9,8},{10,11... | collective-permute-start | bytes 196616 | tf_op jit(solution)/shard_map/ppermute | solution.py:311
  68.8 1.2 collective-permute-start.16
  71.6 6.2 %collective-permute-start.18 = (bf16[5,64,128]{2,1,0:T(8,128)(2,1)S(1)}, bf16[5,64,128]{2,1,0:T(8,128)(2,1)S(1)}, u32[]{:S(2)}, u32[]{:S(2)}) collective-permute-start(bf16[5,64,128]{2,1,0:T(8,128)(2,1)S(1)} %get-tuple-element.67.mine), channel_id=1, source_target_pairs={{0,1},{1,0},{2,3},{3,2},{4,5},{5,4},{6,7},{7,6},{8,9},{9,8},{10,11... | collective-permute-start | bytes 245768 | tf_op jit(solution)/shard_map/ppermute | solution.py:311
  78.8 0.9 collective-permute-start.19
  80.6 6.7 %collective-permute-start.20 = (bf16[5,64,128]{2,1,0:T(8,128)(2,1)S(1)}, bf16[5,64,128]{2,1,0:T(8,128)(2,1)S(1)}, u32[]{:S(2)}, u32[]{:S(2)}) collective-permute-start(bf16[5,64,128]{2,1,0:T(8,128)(2,1)S(1)} %get-tuple-element.69.mine), channel_id=1, source_target_pairs={{0,1},{1,0},{2,3},{3,2},{4,5},{5,4},{6,7},{7,6},{8,9},{9,8},{10,11... | collective-permute-start | bytes 245768 | tf_op jit(solution)/shard_map/ppermute | solution.py:311
  89.8 7.3 %collective-permute-start.22 = (bf16[5,64,128]{2,1,0:T(8,128)(2,1)S(1)}, bf16[5,64,128]{2,1,0:T(8,128)(2,1)S(1)}, u32[]{:S(2)}, u32[]{:S(2)}) collective-permute-start(bf16[5,64,128]{2,1,0:T(8,128)(2,1)S(1)} %get-tuple-element.71.mine), channel_id=1, source_target_pairs={{0,1},{1,0},{2,3},{3,2},{4,5},{5,4},{6,7},{7,6},{8,9},{9,8},{10,11... | collective-permute-start | bytes 245768 | tf_op jit(solution)/shard_map/ppermute | solution.py:311
  99.0 1.3 %collective-permute-start.23 = (f32[128,128]{1,0:T(8,128)S(1)}, f32[128,128]{1,0:T(8,128)S(1)}, u32[]{:S(2)}, u32[]{:S(2)}) collective-permute-start(f32[128,128]{1,0:T(8,128)S(1)} %broadcast_select_fusion.2), channel_id=1, source_target_pairs={{0,1},{1,0},{2,3},{3,2},{4,5},{5,4},{6,7},{7,6},{8,9},{9,8},{10,11... | collective-permute-start | bytes 196616 | tf_op jit(solution)/shard_map/ppermute | solution.py:311
  100.3 5.5 %collective-permute-start.24 = (f32[128,128]{1,0:T(8,128)S(1)}, f32[128,128]{1,0:T(8,128)S(1)}, u32[]{:S(2)}, u32[]{:S(2)}) collective-permute-start(f32[128,128]{1,0:T(8,128)S(1)} %select_add_fusion), channel_id=1, source_target_pairs={{0,2},{1,3},{2,0},{3,1},{4,6},{5,7},{6,4},{7,5},{8,10},{9,11},{10,... | collective-permute-start | bytes 196616 | tf_op jit(solution)/shard_map/ppermute | solution.py:320
  105.9 4.8 %collective-permute-start.25 = (f32[128,128]{1,0:T(8,128)S(1)}, f32[128,128]{1,0:T(8,128)S(1)}, u32[]{:S(2)}, u32[]{:S(2)}) collective-permute-start(f32[128,128]{1,0:T(8,128)S(1)} %add.36), channel_id=1, source_target_pairs={{0,4},{1,5},{2,6},{3,7},{4,0},{5,1},{6,2},{7,3},{8,12},{9,13},{10,... | collective-permute-start | bytes 196616 | tf_op jit(solution)/shard_map/ppermute | solution.py:320
  110.7 5.5 %collective-permute-start.26 = (f32[128,128]{1,0:T(8,128)S(1)}, f32[128,128]{1,0:T(8,128)S(1)}, u32[]{:S(2)}, u32[]{:S(2)}) collective-permute-start(f32[128,128]{1,0:T(8,128)S(1)} %add.37), channel_id=1, source_target_pairs={{0,8},{1,9},{2,10},{3,11},{4,12},{5,13},{6,14},{7,15},{8,0},{9,1},... | collective-permute-start | bytes 196616 | tf_op jit(solution)/shard_map/ppermute | solution.py:320
  116.2 1.3 %collective-permute-start.27 = (f32[128,128]{1,0:T(8,128)S(1)}, f32[128,128]{1,0:T(8,128)S(1)}, u32[]{:S(2)}, u32[]{:S(2)}) collective-permute-start(f32[128,128]{1,0:T(8,128)S(1)} %add.38), channel_id=1, source_target_pairs={{0,1},{1,0},{2,3},{3,2},{4,5},{5,4},{6,7},{7,6},{8,9},{9,8},{10,11... | collective-permute-start | bytes 196616 | tf_op jit(solution)/shard_map/ppermute | solution.py:311
  (8 other events, 9.3 us)
